TPU v7x, 32 devices: a whole 2x2x4 slice. The times are simulated.
32 devices in a mesh: dp: 4 (over y, x), ctx: 8 (over z, core).
Axes of the slice: x: 2, y: 2, z: 4, core: 2. Of those that a mesh axis runs over, the one named last changes fastest.
Arguments:
- queries: bfloat16 [2048, 1024], P('ctx'), may hold values from -12 to 12
- keys: bfloat16 [2048, 128], P('ctx'), may hold values from -5 to 5
- values: bfloat16 [2048, 128], P('ctx'), may hold values from -5 to 5
- out_grad: bfloat16 [2048, 1024], P('ctx'), may hold values from -5 to 5
- segment_ids: int32 [2048], replicated, may hold values from 0 to 3, never falling along the last dimension, each value on 1 to 1792 neighbouring positions
Outputs:
- attn_out: bfloat16 [2048, 1024], P('ctx', 'dp')
- grad_q: bfloat16 [2048, 1024], P('ctx', 'dp')
- grad_k: bfloat16 [2048, 128], P(('dp', 'ctx'))
- grad_v: bfloat16 [2048, 128], P(('dp', 'ctx'))
Inputs may be any that keep to these rules, and one draw needn't show every extreme that they name: `segment_ids`: document numbers never fall along the tokens; each document is a run of positions, the longest exactly 1792.
All inputs are finite; a program needn't handle non-finite values.
Results may differ from a plain program's by a relative error of at most 0.04.
Values may be sent and summed in bfloat16 or wider, within the bound.
No kernel may reach another device: no remote copies, remote signals or barrier semaphores. Data moves between devices by JAX's collectives and lax.ppermute only.
A program may use at most 64 MiB of HBM per device.

v0:
```python
import functools
import math

import jax
import jax.numpy as jnp
from jax import lax
from jax.experimental import pallas as pl
from jax.experimental.pallas import tpu as pltpu
from jax.sharding import PartitionSpec as P

NEG = -1e30
LOG2E = 1.4426950408889634
DOC_NUMBERS = 4
KEY_GROUPS = 2
MIB = 1024 * 1024


def place():
    dp_index, ctx_index = lax.axis_index("dp"), lax.axis_index("ctx")
    return dp_index // KEY_GROUPS, dp_index % KEY_GROUPS, ctx_index // 2, ctx_index % 2

NT = (((1,), (1,)), ((), ()))


def home_chip(spot, key_group, chip, chips):
    level = chips // 4
    flip = spot // level * (2 * level) + spot % level
    home = chip ^ flip
    return home ^ ((home // level % 2) ^ key_group) * level


def gather_rounds(chips):
    if chips == 4:
        first = {(0, 1): (1, 0), (0, 2): (0, 0), (1, 2): (1, 1), (0, 3): (0, 2)}
        return [first, {(0, 3): (0, 0), (1, 3): (1, 1)}]
    rounds = [{} for _ in range(1, chips)]
    for flip, moves in enumerate(rounds, 1):
        for home in range(chips):
            group = home // (chips // 4) % 2
            if home ^ flip > home:
                moves[group, home ^ flip] = (group, home)
    return rounds


def spread_rounds(chips):
    if chips == 4:
        return [{3: 0, 0: 1, 1: 2}, {2: 0, 3: 1, 0: 2, 1: 3}, {1: 0, 2: 1, 3: 2, 0: 3}, {2: 3}]
    return [{chip: chip ^ flip for chip in range(chips)} for flip in range(1, chips)]


def mask_bias(seg_ref, rows, held):
    _, key_group, chip, core = place()
    seg = seg_ref[...]
    lines = rows // 128
    seg_own = seg_ref[pl.ds((chip * 2 + core) * lines, lines), :]
    start = jnp.zeros((lines, 128), jnp.int32)
    for number in range(1, DOC_NUMBERS):
        before = jnp.sum((seg < number).astype(jnp.float32), axis=(0, 1), keepdims=True)
        start = jnp.where(seg_own == number, before.astype(jnp.int32), start)
    start = jnp.concatenate([start[k : k + 1] for k in range(lines)], axis=1)
    query_pos = (chip * 2 + core) * rows + lax.broadcasted_iota(jnp.int32, (1, rows), 1)
    blocks = held // rows
    bias = []
    for block in range(blocks):
        home = home_chip(block // 2, key_group, chip, blocks) * 2 + (core ^ block % 2)
        key_pos = home * rows + lax.broadcasted_iota(jnp.int32, (rows, rows), 0)
        allowed = (key_pos >= start) & (key_pos <= query_pos)
        bias.append(jnp.where(allowed, 0.0, NEG))
    return bias


def load_kernel(k_hbm, v_hbm, kv_ref, sems):
    width = k_hbm.shape[1]
    copies = [
        pltpu.make_async_copy(k_hbm, kv_ref.at[:, :width], sems.at[0]),
        pltpu.make_async_copy(v_hbm, kv_ref.at[:, width:], sems.at[1]),
    ]
    for copy in copies:
        copy.start()
    for copy in copies:
        copy.wait()


def pick_kernel(*refs, choices):
    out_ref = refs[-1]
    _, key_group, chip, _ = place()
    spot = key_group * (len(choices) // 2) + chip
    for choice in sorted(set(choices)):
        wanted = functools.reduce(
            jnp.logical_or, [spot == k for k, c in enumerate(choices) if c == choice]
        )

        @pl.when(wanted)
        def _():
            out_ref[...] = jnp.zeros_like(out_ref) if choice < 0 else refs[choice][...]


def prep_kernel(
    seg_hbm, q_hbm, g_hbm, q_ref, g_ref, gt_ref, bias_ref, token_ref, seg_ref, sems, *, dims
):
    heads, rows, width, held, ctx_count = dims
    head_group = place()[0]
    seg_copy = pltpu.make_async_copy(seg_hbm, seg_ref, sems.at[2, 0])
    seg_copy.start()
    copies = []
    for head in range(heads):
        source = head_columns(head_group * heads + head, width)
        target = slice(head * width, (head + 1) * width)
        for k, (full, part) in enumerate(((g_hbm, g_ref), (q_hbm, q_ref))):
            copies.append(
                pltpu.make_async_copy(full.at[:, source], part.at[:, target], sems.at[k, head])
            )
            copies[-1].start()
    token_ref[...] = jnp.zeros_like(token_ref)
    seg_copy.wait()
    for k, block in enumerate(mask_bias(seg_ref, rows, held)):
        bias_ref[k * rows : (k + 1) * rows, :] = block
    for head in range(heads):
        cols = slice(head * width, (head + 1) * width)
        copies[2 * head].wait()
        gt_ref[cols, :] = g_ref[:, cols].astype(jnp.float32).T.astype(jnp.bfloat16)
    for head in range(heads):
        copies[2 * head + 1].wait()


def head_columns(head, width):
    return pl.ds(pl.multiple_of(head * width, width), width)


def scores_pass(q_ref, bias_ref, blocks, scores_ref, top_ref, *, dims, first):
    heads, rows, width, held, ctx_count = dims
    for head in range(heads):
        query = q_ref[:, head * width : (head + 1) * width]
        top = None
        for k, kv_ref in enumerate(blocks):
            bias = bias_ref[(first + k) * rows : (first + k + 1) * rows, :]
            raw = lax.dot_general(kv_ref[:, :width], query, NT, preferred_element_type=jnp.float32)
            scores = raw * (width**-0.5 * LOG2E) + bias
            scores_ref[head, k * rows : (k + 1) * rows, :] = scores
            here = jnp.max(scores, axis=0, keepdims=True)
            top = here if top is None else jnp.maximum(top, here)
        top_ref[head : head + 1, :] = top


def transpose_values(blocks, vt_ref, width):
    size = blocks[0].shape[0]
    for k, kv_ref in enumerate(blocks):
        vt = kv_ref[:, width:].astype(jnp.float32).T.astype(jnp.bfloat16)
        vt_ref[:, k * size : (k + 1) * size] = vt


def sums_pass(vt_ref, scores_ref, top, head):
    expd = jnp.exp2(scores_ref[head] - top)
    total = jnp.sum(expd, axis=0, keepdims=True)
    sums = jnp.dot(vt_ref[...], expd.astype(jnp.bfloat16), preferred_element_type=jnp.float32)
    return total, sums


def part_kernel(q_ref, bias_ref, *refs, dims):
    heads, rows, width, held, ctx_count = dims
    *blocks, scores_ref, stats_ref, sums_ref, vt_ref = refs
    transpose_values(blocks, vt_ref, width)
    scores_pass(q_ref, bias_ref, blocks, scores_ref, stats_ref, dims=dims, first=0)
    for head in range(heads):
        total, sums_ref[head] = sums_pass(
            vt_ref, scores_ref, stats_ref[head : head + 1, :], head
        )
        stats_ref[heads + head : heads + head + 1, :] = total


def forward_kernel(
    q_ref, gt_ref, bias_ref, kv_ref, part_ref, part_sums_ref, stats_ref, scores_ref, *refs, dims
):
    heads, rows, width, held, ctx_count = dims
    *outs, top_ref, vt_ref = refs
    pair = heads // KEY_GROUPS
    key_group = place()[1]
    transpose_values([kv_ref], vt_ref, width)
    scores_pass(q_ref, bias_ref, [kv_ref], scores_ref, top_ref, dims=dims, first=held // rows - 1)
    for head in range(heads):
        cols = slice(head * width, (head + 1) * width)
        before = part_ref[head : head + 1, :]
        top = jnp.maximum(top_ref[head : head + 1, :], before)
        share = jnp.exp2(before - top)
        total, accum = sums_pass(vt_ref, scores_ref, top, head)
        total = total + share * part_ref[heads + head : heads + head + 1, :]
        accum = accum + share * part_sums_ref[head]
        delta = jnp.sum(accum * gt_ref[cols, :].astype(jnp.float32), axis=0, keepdims=True)
        for row, value in enumerate((top, total, delta)):
            stats_ref[row * heads + head : row * heads + head + 1, :] = value
        where = slice(head % pair * width, (head % pair + 1) * width)
        sums_bf = accum.astype(jnp.bfloat16)
        for slot in range(KEY_GROUPS):

            @pl.when((key_group ^ slot) == head // pair)
            def _():
                outs[slot][where, :] = sums_bf


def dprobs_kernel(g_ref, *refs, dims):
    heads, rows, width, held, ctx_count = dims
    *blocks, dprobs_ref = refs
    for head in range(heads):
        grad = g_ref[:, head * width : (head + 1) * width]
        for part, ref in enumerate(blocks):
            dprobs_ref[head, part * rows : (part + 1) * rows, :] = lax.dot_general(
                ref[:, width:], grad, NT, preferred_element_type=jnp.float32
            )


def merged_stats(stats, heads):
    top = functools.reduce(jnp.maximum, [s[:heads] for s in stats])
    shares = [jnp.exp2(s[:heads] - top) for s in stats]
    total = sum(f * s[heads : 2 * heads] for f, s in zip(shares, stats))
    delta = sum(f * s[2 * heads :] for f, s in zip(shares, stats)) / total
    return top, shares, total, delta


def backward_kernel(q_ref, g_ref, *refs, dims, ahead):
    heads, rows, width, held, ctx_count = dims
    parts = held // rows
    blocks, scores, last_scores, refs = refs[:parts], refs[parts], refs[parts + 1], refs[parts + 2 :]
    dprobs_ref, refs = (refs[0], refs[1:]) if ahead else (None, refs)
    stats = refs[:KEY_GROUPS]
    ds_ref, keep_ref, send_ref, acc_ref = refs[KEY_GROUPS:]
    scale = width**-0.5
    top, _, total, delta = merged_stats([s[...] for s in stats], heads)
    lse = top + jnp.log2(total)
    for head in range(heads):
        cols = slice(head * width, (head + 1) * width)
        query, grad = q_ref[:, cols], g_ref[:, cols]
        for part, ref in enumerate(blocks):
            here = slice(part * rows, (part + 1) * rows)
            row = last_scores[head] if part == parts - 1 else scores[head, here, :]
            probs = jnp.exp2(row - lse[head : head + 1])
            if ahead:
                dprobs = dprobs_ref[head, here, :]
            else:
                dprobs = lax.dot_general(
                    ref[:, width:], grad, NT, preferred_element_type=jnp.float32
                )
            dscores = (probs * (dprobs - delta[head : head + 1])).astype(jnp.bfloat16)
            ds_ref[head, here, :] = dscores
            dv = jnp.dot(probs.astype(jnp.bfloat16), grad, preferred_element_type=jnp.float32)
            dk = jnp.dot(dscores, query, preferred_element_type=jnp.float32)
            if head == 0:
                acc_ref[here, :width] = dk
                acc_ref[here, width:] = dv
            else:
                acc_ref[here, :width] += dk
                acc_ref[here, width:] += dv
    head_group, key_group, chip, core = place()
    chips, piece = ctx_count // 2, rows // 4
    level = chips // 4
    for spot in range(2 * chips):
        here = slice(spot * piece, (spot + 1) * piece)
        target = chip ^ (spot % chips)
        group = head_group ^ (spot // chips)
        block = group * (ctx_count // 2) + key_group * (ctx_count // 4) + target // 2
        flip = block // 2 ^ chip
        slot = flip // (2 * level) * level + flip % level
        line = (slot * 2 + (block % 2 ^ core)) * rows
        for ref, side in ((keep_ref, core), (send_ref, 1 - core)):
            mine = pl.ds(pl.multiple_of(line + (target % 2 * 2 + side) * piece, piece), piece)
            ref[here, :width] = (acc_ref[mine, :width] * scale).astype(ref.dtype)
            ref[here, width:] = acc_ref[mine, width:].astype(ref.dtype)


def query_kernel(*refs, dims):
    heads, rows, width, held, ctx_count = dims
    parts = held // rows
    blocks, ds_ref, refs = refs[:parts], refs[parts], refs[parts + 2 :]
    outs, kt_ref = refs[:KEY_GROUPS], refs[KEY_GROUPS]
    pair = heads // KEY_GROUPS
    key_group = place()[1]
    scale = width**-0.5
    for part, ref in enumerate(blocks):
        here = slice(part * rows, (part + 1) * rows)
        kt_ref[:, here] = ref[:, :width].astype(jnp.float32).T.astype(jnp.bfloat16)
    for slot in range(KEY_GROUPS):
        for part in range(pair):
            head = (key_group ^ slot) * pair + part
            dq = jnp.dot(kt_ref[...], ds_ref[head], preferred_element_type=jnp.float32)
            outs[slot][part * width : (part + 1) * width, :] = (dq * scale).astype(jnp.bfloat16)


def join_kernel(keep_ref, got_ref, kept_ref, send_ref):
    half = kept_ref.shape[0]
    kept_ref[...] = keep_ref[:half, :] + got_ref[:half, :].astype(jnp.float32)
    send = keep_ref[half:, :] + got_ref[half:, :].astype(jnp.float32)
    send_ref[...] = send.astype(jnp.bfloat16)


def spread_kernel(keep_ref, got_ref, token_ref, own_ref, *outs, rounds):
    piece = own_ref.shape[0]
    chip = place()[2]
    own_ref[...] = keep_ref[:piece, :] + got_ref[:piece, :].astype(jnp.float32)
    for out_ref, moves in zip(outs, rounds):
        flip = 0
        for source, target in moves.items():
            flip = jnp.where(chip == source, source ^ target, flip)
        mine = pl.ds(pl.multiple_of(flip * piece, piece), piece)
        out_ref[...] = (keep_ref[mine, :] + got_ref[mine, :].astype(jnp.float32)).astype(
            jnp.bfloat16
        )


def add_kernel(first_ref, second_ref, out_ref):
    out_ref[...] = first_ref[...] + second_ref[...].astype(jnp.float32)


def finish_out_kernel(*refs, dims):
    heads, rows, width, held, ctx_count = dims
    stats, outs = refs[:KEY_GROUPS], refs[KEY_GROUPS : 2 * KEY_GROUPS]
    attn_ref, token_ref = refs[2 * KEY_GROUPS :]
    token_ref[...] = jnp.zeros_like(token_ref)
    pair = heads // KEY_GROUPS
    top, shares, total, _ = merged_stats([s[...] for s in stats], heads)
    own = place()[1] * pair
    row = lax.broadcasted_iota(jnp.int32, (heads, 1), 0)
    for part in range(pair):
        here = slice(part * width, (part + 1) * width)

        def pick(array):
            return jnp.sum(jnp.where(row == own + part, array, 0.0), axis=0, keepdims=True)

        joined = sum(o[here, :].astype(jnp.float32) * pick(f) for o, f in zip(outs, shares))
        attn_ref[:, here] = (joined / pick(total)).T.astype(jnp.bfloat16)


def finish_query_kernel(own_ref, got_ref, gq_ref, token_ref):
    total = own_ref[...].astype(jnp.float32) + got_ref[...].astype(jnp.float32)
    gq_ref[...] = total.T.astype(jnp.bfloat16)
    token_ref[...] = jnp.zeros_like(token_ref)


def finish_kernel(token_ref, *refs):
    *terms, gk_ref, gv_ref = refs
    width = gk_ref.shape[1]
    both = sum(r[...].astype(jnp.float32) for r in terms)
    gk_ref[...] = both[:, :width].astype(jnp.bfloat16)
    gv_ref[...] = both[:, width:].astype(jnp.bfloat16)


def on_device(queries, keys, values, out_grad, segment_ids):
    rows = queries.shape[0]
    width = keys.shape[1]
    seq = segment_ids.shape[0]
    dp_count, ctx_count = lax.axis_size("dp"), lax.axis_size("ctx")
    head_groups = dp_count // KEY_GROUPS
    heads = queries.shape[1] // width // head_groups
    pair = heads // KEY_GROUPS
    chips = ctx_count // 2
    held = rows * ctx_count // KEY_GROUPS
    piece = rows // dp_count
    dims = (heads, rows, width, held, ctx_count)
    seg = segment_ids.reshape(seq // 128, 128)
    params = pltpu.CompilerParams(
        vmem_limit_bytes=min(56 * MIB, 12 * MIB + 12 * 4 * held * rows)
    )
    vmem = pl.BlockSpec(memory_space=pltpu.VMEM)
    bf16, f32 = jnp.bfloat16, jnp.float32

    def call(kernel, outs, ins, name, scratch=(), work=0, **static):
        specs = [a[1] if isinstance(a, tuple) else vmem for a in ins]
        arrays = [a[0] if isinstance(a, tuple) else a for a in ins]
        return pl.pallas_call(
            functools.partial(kernel, **static),
            out_shape=[jax.ShapeDtypeStruct(*o) for o in outs],
            in_specs=specs,
            out_specs=[vmem] * len(outs),
            scratch_shapes=list(scratch),
            compiler_params=params,
            cost_estimate=pl.CostEstimate(
                flops=work * 2 * heads * rows * held * width,
                bytes_accessed=sum(math.prod(o[0]) * 2 for o in outs),
                transcendentals=0,
            ),
            name=name,
        )(*arrays)

    def in_hbm(array):
        return pltpu.with_memory_space_constraint(array, pltpu.HBM), pl.BlockSpec(
            memory_space=pltpu.HBM
        )

    def over_dp(array, flip):
        return lax.ppermute(array, "dp", [(d, d ^ flip) for d in range(dp_count)])

    def over_cores(array):
        return lax.ppermute(array, "ctx", [(c, c ^ 1) for c in range(ctx_count)])

    def gathered(array, moves):
        pairs = []
        for d in range(0, dp_count, KEY_GROUPS):
            for (group, chip), (source, home) in moves.items():
                for core in range(2):
                    start = (d + source) * ctx_count + home * 2 + core
                    pairs.append((start, (d + group) * ctx_count + chip * 2 + core))
        return lax.ppermute(array, ("dp", "ctx"), pairs)

    def spread(array, moves):
        pairs = [(a * 2 + core, b * 2 + core) for a, b in moves.items() for core in range(2)]
        return lax.ppermute(array, "ctx", pairs)

    (own_kv,) = call(
        load_kernel,
        [((rows, 2 * width), bf16)],
        [in_hbm(keys), in_hbm(values)],
        "load",
        scratch=[pltpu.SemaphoreType.DMA((2,))],
    )
    query_v, grad_v, grad_t, bias, token = call(
        prep_kernel,
        [
            ((rows, heads * width), bf16),
            ((rows, heads * width), bf16),
            ((heads * width, rows), bf16),
            ((held, rows), f32),
            ((8, 128), f32),
        ],
        [in_hbm(seg), in_hbm(queries), in_hbm(out_grad)],
        "prepare",
        scratch=[pltpu.VMEM(seg.shape, seg.dtype), pltpu.SemaphoreType.DMA((3, heads))],
        work=1,
        dims=dims,
    )
    rounds = gather_rounds(chips)
    sent = [own_kv] + [gathered(own_kv, moves) for moves in rounds]
    blocks = []
    for spot in range(chips // 2):
        choices = []
        for group in range(KEY_GROUPS):
            for chip in range(chips):
                home = home_chip(spot, group, chip, chips)
                ways = [k for k, moves in enumerate(rounds, 1) if moves.get((group, chip), (0, chip))[1] == home]
                choices.append(0 if home == chip else ways[0] if home < chip else -1)
        used = sorted(set(choices) - {-1})
        (picked,) = call(
            pick_kernel,
            [((rows, 2 * width), bf16)],
            [sent[k] for k in used] + [token],
            "pick",
            choices=[used.index(c) if c >= 0 else -1 for c in choices],
        )
        blocks += [picked, over_cores(picked)]
    early = held - rows
    scores, part_stats, part_sums = call(
        part_kernel,
        [((heads, early, rows), f32), ((2 * heads, rows), f32), ((heads, width, rows), f32)],
        [query_v, bias] + blocks[:-1],
        "attend_most",
        scratch=[pltpu.VMEM((width, early), bf16)],
        work=2,
        dims=dims,
    )
    stats, last_scores, *outs = call(
        forward_kernel,
        [((3 * heads, rows), f32), ((heads, rows, rows), f32)]
        + [((pair * width, rows), bf16)] * KEY_GROUPS,
        [query_v, grad_t, bias, blocks[-1], part_stats, part_sums],
        "attend",
        scratch=[pltpu.VMEM((heads, rows), f32), pltpu.VMEM((width, rows), bf16)],
        work=1,
        dims=dims,
    )
    all_stats = [stats, over_dp(stats, 1)]
    all_outs = [outs[0], over_dp(outs[1], 1)]
    ahead = 4 * heads * held * rows <= 8 * MIB
    dprobs = []
    if ahead:
        dprobs = call(
            dprobs_kernel,
            [((heads, held, rows), f32)],
            [grad_v] + blocks,
            "dprobs",
            work=1,
            dims=dims,
        )

    dscores, keep, send = call(
        backward_kernel,
        [
            ((heads, held, rows), bf16),
            ((held // 2, 2 * width), f32),
            ((held // 2, 2 * width), bf16),
        ],
        [query_v, grad_v] + blocks + [scores, last_scores] + list(dprobs) + all_stats,
        "differentiate",
        scratch=[pltpu.VMEM((held, 2 * width), f32)],
        work=4,
        dims=dims,
        ahead=ahead,
    )
    got = over_cores(send)
    attn_out, token = call(
        finish_out_kernel,
        [((rows, pair * width), bf16), ((8, 128), f32)],
        all_stats + all_outs,
        "finish_out",
        dims=dims,
    )
    quarter = held // 4
    keep, send = call(
        join_kernel,
        [((quarter, 2 * width), f32), ((quarter, 2 * width), bf16)],
        [keep, got],
        "join_cores",
    )
    dqs = call(
        query_kernel,
        [((pair * width, rows), bf16)] * KEY_GROUPS,
        blocks + [dscores, keep],
        "query_terms",
        scratch=[pltpu.VMEM((width, held), bf16)],
        work=1,
        dims=dims,
    )
    all_dqs = [dqs[0], over_dp(dqs[1], 1)]
    rounds = spread_rounds(chips)
    terms, *pieces = call(
        spread_kernel,
        [((piece, 2 * width), f32)] + [((piece, 2 * width), bf16)] * len(rounds),
        [keep, over_dp(send, 2), token],
        "join_heads",
        rounds=rounds,
    )
    got = [spread(p, moves) for p, moves in zip(pieces, rounds)]
    for array in got[:-1]:
        (terms,) = call(add_kernel, [((piece, 2 * width), f32)], [terms, array], "add_terms")

    grad_q, token = call(
        finish_query_kernel,
        [((rows, pair * width), bf16), ((8, 128), f32)],
        all_dqs,
        "finish_query",
    )
    grad_k, grad_values = call(
        finish_kernel, [((piece, width), bf16)] * 2, [token, terms, got[-1]], "finish"
    )
    return attn_out, grad_q, grad_k, grad_values


def solution(mesh):
    return jax.shard_map(
        on_device,
        mesh=mesh,
        in_specs=(P("ctx", None), P("ctx", None), P("ctx", None), P("ctx", None), P()),
        out_specs=(P("ctx", "dp"), P("ctx", "dp"), P(("dp", "ctx"), None), P(("dp", "ctx"), None)),
        check_vma=False,
    )
```

profile of v0, /device:TPU:0, one launch (start us, length us, event | category | flops | bytes accessed | tf_op | source)
XLA Modules:
  0.0 37.6 jit_solution(8167168604989346254)
XLA Ops:
  0.6 0.9 %load.1.refs_0_ = bf16[256,256]{1,0:T(8,128)(2,1)S(1)} custom-call(bf16[256,128]{1,0:T(8,128)(2,1)} %k_hbm.1, bf16[256,128]{1,0:T(8,128)(2,1)} %v_hbm.1), custom_call_target="tpu_custom_call" | custom-call | bytes 131072 | tf_op jit(solution)/shard_map/load/pallas_call | solution.py:367
  1.5 5.9 %collective-permute-start = (bf16[256,256]{1,0:T(8,128)(2,1)S(1)}, bf16[256,256]{1,0:T(8,128)(2,1)S(1)}, u32[]{:S(2)}, u32[]{:S(2)}) collective-permute-start(bf16[256,256]{1,0:T(8,128)(2,1)S(1)} %load.1.refs_0_), channel_id=1, source_target_pairs={{8,2},{9,3},{0,4},{1,5},{10,12},{11,13},{4,6},{5,7},{24,18},{25,19... | collective-permute-start | bytes 393224 | tf_op jit(solution)/shard_map/ppermute | solution.py:400
  7.5 2.3 %collective-permute-start.1 = (bf16[256,256]{1,0:T(8,128)(2,1)S(1)}, bf16[256,256]{1,0:T(8,128)(2,1)S(1)}, u32[]{:S(2)}, u32[]{:S(2)}) collective-permute-start(bf16[256,256]{1,0:T(8,128)(2,1)S(1)} %load.1.refs_0_), channel_id=1, source_target_pairs={{0,6},{1,7},{10,14},{11,15},{16,22},{17,23},{26,30},{27,31}} | collective-permute-start | bytes 393224 | tf_op jit(solution)/shard_map/ppermute | solution.py:400
  9.8 1.5 %prepare.1 = (bf16[256,512]{1,0:T(8,128)(2,1)S(1)}, bf16[256,512]{1,0:T(8,128)(2,1)S(1)}, bf16[512,256]{1,0:T(8,128)(2,1)S(1)}, f32[1024,256]{1,0:T(8,128)S(1)}, f32[8,128]{1,0:T(8,128)S(1)}) custom-call(s32[16,128]{1,0:T(8,128)} %bitcast.1, bf16[256,1024]{1,0:T(8,128)(2,1)} %q_hbm.1, bf16[256,1024]{1,0:T(8,128)(2,1)} %g_hbm.1), custom_call_target="tpu_custom_call" | custom-call | flops 268435456 | bytes 1312768 | tf_op jit(solution)/shard_map/prepare/pallas_call | solution.py:367
  11.3 0.0 collective-permute-done.refs_0_.refs_1_
  11.4 0.1 collective-permute-start.3
  11.4 1.6 %collective-permute-done.1.refs_1_ = bf16[256,256]{1,0:T(8,128)(2,1)S(1)} collective-permute-done((bf16[256,256]{1,0:T(8,128)(2,1)S(1)}, bf16[256,256]{1,0:T(8,128)(2,1)S(1)}, u32[]{:S(2)}, u32[]{:S(2)}) %collective-permute-start.1) | collective-permute-done | bytes 131104 | tf_op jit(solution)/shard_map/ppermute | solution.py:400
  13.0 0.1 collective-permute-start.2
  13.1 0.0 collective-permute-done.3.refs_1_
  13.1 1.2 %attend_most.1 = (f32[4,768,256]{2,1,0:T(8,128)S(1)}, f32[8,256]{1,0:T(8,128)S(1)}, f32[4,128,256]{2,1,0:T(8,128)S(1)}) custom-call(bf16[256,512]{1,0:T(8,128)(2,1)S(1)} %get-tuple-element.34.q_ref, f32[1024,256]{1,0:T(8,128)S(1)} %get-tuple-element.36.bias_ref, bf16[256,256]{1,0:T(8,128)(2,1)S(1)} %pick.3.refs_0_, ...), custom_call_target="tpu_custom_call" | custom-call | flops 536870912 | bytes 1839104 | tf_op jit(solution)/shard_map/attend_most/pallas_call | solution.py:367
  14.3 0.1 collective-permute-done.2.kv_ref.refs_3_
  14.5 1.1 %attend.1 = (f32[12,256]{1,0:T(8,128)S(1)}, f32[4,256,256]{2,1,0:T(8,128)S(1)}, bf16[256,256]{1,0:T(8,128)(2,1)S(1)}, bf16[256,256]{1,0:T(8,128)(2,1)S(1)}) custom-call(bf16[256,512]{1,0:T(8,128)(2,1)S(1)} %get-tuple-element.34.q_ref, bf16[512,256]{1,0:T(8,128)(2,1)S(1)} %get-tuple-element.35.gt_ref, f32[1024,256]{1,0:T(8,128)S(1)} %get-tuple-element.36.bias_ref, ...), custom_call_target="tpu_custom_call" | custom-call | flops 268435456 | bytes 792576 | tf_op jit(solution)/shard_map/attend/pallas_call | solution.py:367
  15.6 0.1 collective-permute-start.4
  15.7 0.7 %dprobs.1.refs_6_ = f32[4,1024,256]{2,1,0:T(8,128)S(1)} custom-call(bf16[256,512]{1,0:T(8,128)(2,1)S(1)} %get-tuple-element.44.g_ref, bf16[256,256]{1,0:T(8,128)(2,1)S(1)} %pick.3.refs_0_, bf16[256,256]{1,0:T(8,128)(2,1)S(1)} %collective-permute-done.3.refs_1_, bf16[256,256]{1,0:T(8,128)(2,1)S(1)} %pick.2.refs_2_, ...), custom_call_target="tpu_custom_call" | custom-call | flops 268435456 | bytes 2097152 | tf_op jit(solution)/shard_map/dprobs/pallas_call | solution.py:367
  16.4 3.0 %collective-permute-done.4.refs_1_.refs_8_ = f32[12,256]{1,0:T(8,128)S(1)} collective-permute-done((f32[12,256]{1,0:T(8,128)S(1)}, f32[12,256]{1,0:T(8,128)S(1)}, u32[]{:S(2)}, u32[]{:S(2)}) %collective-permute-start.4) | collective-permute-done | bytes 12320 | tf_op jit(solution)/shard_map/ppermute | solution.py:388
  19.4 1.6 %differentiate.1 = (bf16[4,1024,256]{2,1,0:T(8,128)(2,1)S(1)}, f32[512,256]{1,0:T(8,128)S(1)}, bf16[512,256]{1,0:T(8,128)(2,1)S(1)}) custom-call(bf16[256,512]{1,0:T(8,128)(2,1)S(1)} %get-tuple-element.34.q_ref, bf16[256,512]{1,0:T(8,128)(2,1)S(1)} %get-tuple-element.44.g_ref, bf16[256,256]{1,0:T(8,128)(2,1)S(1)} %pick.3.refs_0_, ...), custom_call_target="tpu_custom_call" | custom-call | flops 1073741824 | bytes 2621440 | tf_op jit(solution)/shard_map/differentiate/pallas_call | solution.py:367
  21.0 0.1 collective-permute-start.6
  21.1 0.1 collective-permute-start.5
  21.1 1.4 %collective-permute-done.6.got_ref = bf16[512,256]{1,0:T(8,128)(2,1)S(1)} collective-permute-done((bf16[512,256]{1,0:T(8,128)(2,1)S(1)}, bf16[512,256]{1,0:T(8,128)(2,1)S(1)}, u32[]{:S(2)}, u32[]{:S(2)}) %collective-permute-start.6) | collective-permute-done | bytes 262176 | tf_op jit(solution)/shard_map/ppermute | solution.py:391
  22.6 1.6 %collective-permute-start.8 = (bf16[256,256]{1,0:T(8,128)(2,1)S(1)}, bf16[256,256]{1,0:T(8,128)(2,1)S(1)}, u32[]{:S(2)}, u32[]{:S(2)}) collective-permute-start(bf16[256,256]{1,0:T(8,128)(2,1)S(1)} %get-tuple-element.55), channel_id=1, source_target_pairs={{0,16},{8,24},{16,0},{24,8},{1,17},{9,25},{17,1},{25,9},{2,18},{10... | collective-permute-start | bytes 393224 | tf_op jit(solution)/shard_map/ppermute | solution.py:388
  24.2 0.5 %query_terms.1 = (bf16[256,256]{1,0:T(8,128)(2,1)S(1)}, bf16[256,256]{1,0:T(8,128)(2,1)S(1)}) custom-call(bf16[256,256]{1,0:T(8,128)(2,1)S(1)} %pick.3.refs_0_, bf16[256,256]{1,0:T(8,128)(2,1)S(1)} %collective-permute-done.3.refs_1_, bf16[256,256]{1,0:T(8,128)(2,1)S(1)} %pick.2.refs_2_, bf16[256,256]{1,0:T(8,128)(2,1)S(1)} %collective-permute-done.2.kv_ref.refs_3_, ...), custom_call_target="tpu_custom_call" | custom-call | flops 268435456 | bytes 262144 | tf_op jit(solution)/shard_map/query_terms/pallas_call | solution.py:367
  24.7 0.6 %collective-permute-start.7 = (bf16[256,256]{1,0:T(8,128)(2,1)S(1)}, bf16[256,256]{1,0:T(8,128)(2,1)S(1)}, u32[]{:S(2)}, u32[]{:S(2)}) collective-permute-start(bf16[256,256]{1,0:T(8,128)(2,1)S(1)} %get-tuple-element.52), channel_id=1, source_target_pairs={{0,8},{8,0},{16,24},{24,16},{1,9},{9,1},{17,25},{25,17},{2,10},{10... | collective-permute-start | bytes 393224 | tf_op jit(solution)/shard_map/ppermute | solution.py:388
  25.3 1.6 %collective-permute-done.5.refs_3_ = bf16[256,256]{1,0:T(8,128)(2,1)S(1)} collective-permute-done((bf16[256,256]{1,0:T(8,128)(2,1)S(1)}, bf16[256,256]{1,0:T(8,128)(2,1)S(1)}, u32[]{:S(2)}, u32[]{:S(2)}) %collective-permute-start.5) | collective-permute-done | bytes 131104 | tf_op jit(solution)/shard_map/ppermute | solution.py:388
  27.0 0.8 %finish_out.1 = (bf16[256,256]{1,0:T(8,128)(2,1)}, f32[8,128]{1,0:T(8,128)S(1)}) custom-call(f32[12,256]{1,0:T(8,128)S(1)} %get-tuple-element.40.refs_0_.refs_7_, f32[12,256]{1,0:T(8,128)S(1)} %collective-permute-done.4.refs_1_.refs_8_, bf16[256,256]{1,0:T(8,128)(2,1)S(1)} %get-tuple-element.41.refs_2_, bf16[256,256]{1,0:T(8,128)(2,1)S(1)} %collective-permute-done.5.refs_3_), custom_call_target="tpu_custom_call" | custom-call | bytes 133120 | tf_op jit(solution)/shard_map/finish_out/pallas_call | solution.py:367
  27.8 0.4 %collective-permute-done.8.got_ref = bf16[256,256]{1,0:T(8,128)(2,1)S(1)} collective-permute-done((bf16[256,256]{1,0:T(8,128)(2,1)S(1)}, bf16[256,256]{1,0:T(8,128)(2,1)S(1)}, u32[]{:S(2)}, u32[]{:S(2)}) %collective-permute-start.8) | collective-permute-done | bytes 131104 | tf_op jit(solution)/shard_map/ppermute | solution.py:388
  28.3 2.6 %collective-permute-start.9 = (bf16[64,256]{1,0:T(8,128)(2,1)S(1)}, bf16[64,256]{1,0:T(8,128)(2,1)S(1)}, u32[]{:S(2)}, u32[]{:S(2)}) collective-permute-start(bf16[64,256]{1,0:T(8,128)(2,1)S(1)} %get-tuple-element.58), channel_id=1, source_target_pairs={{6,0},{7,1},{0,2},{1,3},{2,4},{3,5},{14,8},{15,9},{8,10},{9,11},{1... | collective-permute-start | bytes 98312 | tf_op jit(solution)/shard_map/ppermute | solution.py:404
  30.9 0.9 %collective-permute-start.10 = (bf16[64,256]{1,0:T(8,128)(2,1)S(1)}, bf16[64,256]{1,0:T(8,128)(2,1)S(1)}, u32[]{:S(2)}, u32[]{:S(2)}) collective-permute-start(bf16[64,256]{1,0:T(8,128)(2,1)S(1)} %get-tuple-element.59), channel_id=1, source_target_pairs={{4,0},{5,1},{6,2},{7,3},{0,4},{1,5},{2,6},{3,7},{12,8},{13,9},{14,... | collective-permute-start | bytes 98312 | tf_op jit(solution)/shard_map/ppermute | solution.py:404
  31.9 3.5 %collective-permute-start.11 = (bf16[64,256]{1,0:T(8,128)(2,1)S(1)}, bf16[64,256]{1,0:T(8,128)(2,1)S(1)}, u32[]{:S(2)}, u32[]{:S(2)}) collective-permute-start(bf16[64,256]{1,0:T(8,128)(2,1)S(1)} %get-tuple-element.60), channel_id=1, source_target_pairs={{2,0},{3,1},{4,2},{5,3},{6,4},{7,5},{0,6},{1,7},{10,8},{11,9},{12,... | collective-permute-start | bytes 98312 | tf_op jit(solution)/shard_map/ppermute | solution.py:404
  35.4 0.7 %collective-permute-start.12 = (bf16[64,256]{1,0:T(8,128)(2,1)S(1)}, bf16[64,256]{1,0:T(8,128)(2,1)S(1)}, u32[]{:S(2)}, u32[]{:S(2)}) collective-permute-start(bf16[64,256]{1,0:T(8,128)(2,1)S(1)} %get-tuple-element.61), channel_id=1, source_target_pairs={{4,6},{5,7},{12,14},{13,15},{20,22},{21,23},{28,30},{29,31}} | collective-permute-start | bytes 98312 | tf_op jit(solution)/shard_map/ppermute | solution.py:404
  36.1 0.0 collective-permute-done.7.got_ref
  36.1 0.8 %finish_query.1 = (bf16[256,256]{1,0:T(8,128)(2,1)}, f32[8,128]{1,0:T(8,128)S(1)}) custom-call(bf16[256,256]{1,0:T(8,128)(2,1)S(1)} %get-tuple-element.51.own_ref, bf16[256,256]{1,0:T(8,128)(2,1)S(1)} %collective-permute-done.7.got_ref), custom_call_target="tpu_custom_call" | custom-call | bytes 133120 | tf_op jit(solution)/shard_map/finish_query/pallas_call | solution.py:367
  36.8 0.0 collective-permute-done.9.second_ref
  36.9 0.0 collective-permute-done.10.second_ref
  36.9 0.1 collective-permute-done.11.second_ref
  37.0 0.0 collective-permute-done.12.refs_1_
  37.0 0.6 %finish.1 = (bf16[64,128]{1,0:T(8,128)(2,1)}, bf16[64,128]{1,0:T(8,128)(2,1)}) custom-call(f32[8,128]{1,0:T(8,128)S(1)} %get-tuple-element.54.token_ref, f32[64,256]{1,0:T(8,128)S(1)} %add_terms.5.refs_0_, bf16[64,256]{1,0:T(8,128)(2,1)S(1)} %collective-permute-done.12.refs_1_), custom_call_target="tpu_custom_call" | custom-call | bytes 32768 | tf_op jit(solution)/shard_map/finish/pallas_call | solution.py:367
  (7 shorter events, 0.2 us)
Async XLA Ops:
  1.5 9.8 %collective-permute-start = (bf16[256,256]{1,0:T(8,128)(2,1)S(1)}, bf16[256,256]{1,0:T(8,128)(2,1)S(1)}, u32[]{:S(2)}, u32[]{:S(2)}) collective-permute-start(bf16[256,256]{1,0:T(8,128)(2,1)S(1)} %load.1.refs_0_), channel_id=1, source_target_pairs={{8,2},{9,3},{0,4},{1,5},{10,12},{11,13},{4,6},{5,7},{24,18},{25,19... | collective-permute-start | bytes 393224 | tf_op jit(solution)/shard_map/ppermute | solution.py:400
  7.5 5.5 %collective-permute-start.1 = (bf16[256,256]{1,0:T(8,128)(2,1)S(1)}, bf16[256,256]{1,0:T(8,128)(2,1)S(1)}, u32[]{:S(2)}, u32[]{:S(2)}) collective-permute-start(bf16[256,256]{1,0:T(8,128)(2,1)S(1)} %load.1.refs_0_), channel_id=1, source_target_pairs={{0,6},{1,7},{10,14},{11,15},{16,22},{17,23},{26,30},{27,31}} | collective-permute-start | bytes 393224 | tf_op jit(solution)/shard_map/ppermute | solution.py:400
  11.4 1.8 %collective-permute-start.3 = (bf16[256,256]{1,0:T(8,128)(2,1)S(1)}, bf16[256,256]{1,0:T(8,128)(2,1)S(1)}, u32[]{:S(2)}, u32[]{:S(2)}) collective-permute-start(bf16[256,256]{1,0:T(8,128)(2,1)S(1)} %pick.3.refs_0_), channel_id=1, source_target_pairs={{0,1},{1,0},{2,3},{3,2},{4,5},{5,4},{6,7},{7,6},{8,9},{9,8},{10,11... | collective-permute-start | bytes 393224 | tf_op jit(solution)/shard_map/ppermute | solution.py:391
  13.0 1.4 %collective-permute-start.2 = (bf16[256,256]{1,0:T(8,128)(2,1)S(1)}, bf16[256,256]{1,0:T(8,128)(2,1)S(1)}, u32[]{:S(2)}, u32[]{:S(2)}) collective-permute-start(bf16[256,256]{1,0:T(8,128)(2,1)S(1)} %pick.2.refs_2_), channel_id=1, source_target_pairs={{0,1},{1,0},{2,3},{3,2},{4,5},{5,4},{6,7},{7,6},{8,9},{9,8},{10,11... | collective-permute-start | bytes 393224 | tf_op jit(solution)/shard_map/ppermute | solution.py:391
  15.6 3.8 %collective-permute-start.4 = (f32[12,256]{1,0:T(8,128)S(1)}, f32[12,256]{1,0:T(8,128)S(1)}, u32[]{:S(2)}, u32[]{:S(2)}) collective-permute-start(f32[12,256]{1,0:T(8,128)S(1)} %get-tuple-element.40.refs_0_.refs_7_), channel_id=1, source_target_pairs={{0,8},{8,0},{16,24},{24,16},{1,9},{9,1},{17,25},{25,17},{2,10},{10... | collective-permute-start | bytes 36872 | tf_op jit(solution)/shard_map/ppermute | solution.py:388
  21.0 1.6 %collective-permute-start.6 = (bf16[512,256]{1,0:T(8,128)(2,1)S(1)}, bf16[512,256]{1,0:T(8,128)(2,1)S(1)}, u32[]{:S(2)}, u32[]{:S(2)}) collective-permute-start(bf16[512,256]{1,0:T(8,128)(2,1)S(1)} %get-tuple-element.49), channel_id=1, source_target_pairs={{0,1},{1,0},{2,3},{3,2},{4,5},{5,4},{6,7},{7,6},{8,9},{9,8},{10,11... | collective-permute-start | bytes 786440 | tf_op jit(solution)/shard_map/ppermute | solution.py:391
  21.1 5.9 %collective-permute-start.5 = (bf16[256,256]{1,0:T(8,128)(2,1)S(1)}, bf16[256,256]{1,0:T(8,128)(2,1)S(1)}, u32[]{:S(2)}, u32[]{:S(2)}) collective-permute-start(bf16[256,256]{1,0:T(8,128)(2,1)S(1)} %get-tuple-element.42), channel_id=1, source_target_pairs={{0,8},{8,0},{16,24},{24,16},{1,9},{9,1},{17,25},{25,17},{2,10},{10... | collective-permute-start | bytes 393224 | tf_op jit(solution)/shard_map/ppermute | solution.py:388
  22.6 5.6 %collective-permute-start.8 = (bf16[256,256]{1,0:T(8,128)(2,1)S(1)}, bf16[256,256]{1,0:T(8,128)(2,1)S(1)}, u32[]{:S(2)}, u32[]{:S(2)}) collective-permute-start(bf16[256,256]{1,0:T(8,128)(2,1)S(1)} %get-tuple-element.55), channel_id=1, source_target_pairs={{0,16},{8,24},{16,0},{24,8},{1,17},{9,25},{17,1},{25,9},{2,18},{10... | collective-permute-start | bytes 393224 | tf_op jit(solution)/shard_map/ppermute | solution.py:388
  24.7 11.4 %collective-permute-start.7 = (bf16[256,256]{1,0:T(8,128)(2,1)S(1)}, bf16[256,256]{1,0:T(8,128)(2,1)S(1)}, u32[]{:S(2)}, u32[]{:S(2)}) collective-permute-start(bf16[256,256]{1,0:T(8,128)(2,1)S(1)} %get-tuple-element.52), channel_id=1, source_target_pairs={{0,8},{8,0},{16,24},{24,16},{1,9},{9,1},{17,25},{25,17},{2,10},{10... | collective-permute-start | bytes 393224 | tf_op jit(solution)/shard_map/ppermute | solution.py:388
  28.3 8.6 %collective-permute-start.9 = (bf16[64,256]{1,0:T(8,128)(2,1)S(1)}, bf16[64,256]{1,0:T(8,128)(2,1)S(1)}, u32[]{:S(2)}, u32[]{:S(2)}) collective-permute-start(bf16[64,256]{1,0:T(8,128)(2,1)S(1)} %get-tuple-element.58), channel_id=1, source_target_pairs={{6,0},{7,1},{0,2},{1,3},{2,4},{3,5},{14,8},{15,9},{8,10},{9,11},{1... | collective-permute-start | bytes 98312 | tf_op jit(solution)/shard_map/ppermute | solution.py:404
  30.9 5.9 %collective-permute-start.10 = (bf16[64,256]{1,0:T(8,128)(2,1)S(1)}, bf16[64,256]{1,0:T(8,128)(2,1)S(1)}, u32[]{:S(2)}, u32[]{:S(2)}) collective-permute-start(bf16[64,256]{1,0:T(8,128)(2,1)S(1)} %get-tuple-element.59), channel_id=1, source_target_pairs={{4,0},{5,1},{6,2},{7,3},{0,4},{1,5},{2,6},{3,7},{12,8},{13,9},{14,... | collective-permute-start | bytes 98312 | tf_op jit(solution)/shard_map/ppermute | solution.py:404
  31.9 5.1 %collective-permute-start.11 = (bf16[64,256]{1,0:T(8,128)(2,1)S(1)}, bf16[64,256]{1,0:T(8,128)(2,1)S(1)}, u32[]{:S(2)}, u32[]{:S(2)}) collective-permute-start(bf16[64,256]{1,0:T(8,128)(2,1)S(1)} %get-tuple-element.60), channel_id=1, source_target_pairs={{2,0},{3,1},{4,2},{5,3},{6,4},{7,5},{0,6},{1,7},{10,8},{11,9},{12,... | collective-permute-start | bytes 98312 | tf_op jit(solution)/shard_map/ppermute | solution.py:404
  35.4 1.6 %collective-permute-start.12 = (bf16[64,256]{1,0:T(8,128)(2,1)S(1)}, bf16[64,256]{1,0:T(8,128)(2,1)S(1)}, u32[]{:S(2)}, u32[]{:S(2)}) collective-permute-start(bf16[64,256]{1,0:T(8,128)(2,1)S(1)} %get-tuple-element.61), channel_id=1, source_target_pairs={{4,6},{5,7},{12,14},{13,15},{20,22},{21,23},{28,30},{29,31}} | collective-permute-start | bytes 98312 | tf_op jit(solution)/shard_map/ppermute | solution.py:404
where the time goes:
time: 37.9 us; the launch traced here: 37.6 us
  starting transfers between devices  18.6 us (49%)
  Pallas kernels  9.84 us (26%)
  waiting for transfers between devices  8.41 us (22%)
  between operations  0.83 us (2%)
    pallas_call x17, Pallas kernels, call(): pl.pallas_call(functools.partial(kernel, **static), out_shape=[jax.ShapeD...  9.84 us
    ppermute x2, starting transfers between devices, gathered(): return lax.ppermute(array, ('dp', 'ctx'), pairs)  8.25 us
    ppermute x4, starting transfers between devices, spread(): return lax.ppermute(array, 'ctx', pairs)  7.76 us
    ppermute x4, waiting for transfers between devices, over_dp(): return lax.ppermute(array, 'dp', [(d, d ^ flip) for d in range(dp_count)])  5.12 us
    ppermute x4, starting transfers between devices, over_dp(): return lax.ppermute(array, 'dp', [(d, d ^ flip) for d in range(dp_count)])  2.35 us
    ppermute x3, waiting for transfers between devices, over_cores(): return lax.ppermute(array, 'ctx', [(c, c ^ 1) for c in range(ctx_count)])  1.58 us
    ppermute x2, waiting for transfers between devices, gathered(): return lax.ppermute(array, ('dp', 'ctx'), pairs)  1.58 us
  transfers between devices with their start and end apart: 13, of which 7 were waited for; matrix products, arithmetic and copies ran while one was open for 0% of the time, Pallas kernels for 15%

commit v1 on v0

--- a/solution.py
+++ b/solution.py
@@ -30,22 +30,26 @@
 
 
 def gather_rounds(chips):
-    if chips == 4:
-        first = {(0, 1): (1, 0), (0, 2): (0, 0), (1, 2): (1, 1), (0, 3): (0, 2)}
-        return [first, {(0, 3): (0, 0), (1, 3): (1, 1)}]
-    rounds = [{} for _ in range(1, chips)]
-    for flip, moves in enumerate(rounds, 1):
-        for home in range(chips):
-            group = home // (chips // 4) % 2
-            if home ^ flip > home:
-                moves[group, home ^ flip] = (group, home)
+    rounds = [{} for _ in range(2 if chips == 4 else chips - 1)]
+    for core in range(2):
+        if chips == 4:
+            rounds[0][0, 1, core] = (1, 0)
+            rounds[0][0, 2, core] = (0, 0)
+            rounds[0][1, 2, core] = (1, 1)
+            rounds[0][0, 3, core] = (core, 2)
+            rounds[1][0, 3, core] = (0, 0)
+            rounds[1][1, 3, core] = (1, 1)
+            continue
+        for flip, moves in enumerate(rounds, 1):
+            for home in range(chips):
+                group = home // (chips // 4) % 2
+                if home ^ flip > home:
+                    moves[group, home ^ flip, core] = (group, home)
     return rounds
 
 
 def spread_rounds(chips):
-    if chips == 4:
-        return [{3: 0, 0: 1, 1: 2}, {2: 0, 3: 1, 0: 2, 1: 3}, {1: 0, 2: 1, 3: 2, 0: 3}, {2: 3}]
-    return [{chip: chip ^ flip for chip in range(chips)} for flip in range(1, chips)]
+    return [{chip: (chip + step) % chips for chip in range(chips)} for step in range(1, chips)]
 
 
 def mask_bias(seg_ref, rows, held):
@@ -172,7 +176,7 @@
     q_ref, gt_ref, bias_ref, kv_ref, part_ref, part_sums_ref, stats_ref, scores_ref, *refs, dims
 ):
     heads, rows, width, held, ctx_count = dims
-    *outs, top_ref, vt_ref = refs
+    *outs, top_ref, vt_ref, sums_ref = refs
     pair = heads // KEY_GROUPS
     key_group = place()[1]
     transpose_values([kv_ref], vt_ref, width)
@@ -188,13 +192,9 @@
         delta = jnp.sum(accum * gt_ref[cols, :].astype(jnp.float32), axis=0, keepdims=True)
         for row, value in enumerate((top, total, delta)):
             stats_ref[row * heads + head : row * heads + head + 1, :] = value
-        where = slice(head % pair * width, (head % pair + 1) * width)
-        sums_bf = accum.astype(jnp.bfloat16)
-        for slot in range(KEY_GROUPS):
-
-            @pl.when((key_group ^ slot) == head // pair)
-            def _():
-                outs[slot][where, :] = sums_bf
+        sums_ref[cols, :] = accum.astype(jnp.bfloat16)
+    for slot, out_ref in enumerate(outs):
+        out_ref[...] = sums_ref[head_columns(key_group ^ slot, pair * width), :]
 
 
 def dprobs_kernel(g_ref, *refs, dims):
@@ -328,13 +328,13 @@
         attn_ref[:, here] = (joined / pick(total)).T.astype(jnp.bfloat16)
 
 
-def finish_query_kernel(own_ref, got_ref, gq_ref, token_ref):
+def finish_query_kernel(own_ref, got_ref, piece_ref, gq_ref, passed_ref):
     total = own_ref[...].astype(jnp.float32) + got_ref[...].astype(jnp.float32)
     gq_ref[...] = total.T.astype(jnp.bfloat16)
-    token_ref[...] = jnp.zeros_like(token_ref)
-
-
-def finish_kernel(token_ref, *refs):
+    passed_ref[...] = piece_ref[...]
+
+
+def finish_kernel(*refs):
     *terms, gk_ref, gv_ref = refs
     width = gk_ref.shape[1]
     both = sum(r[...].astype(jnp.float32) for r in terms)
@@ -393,10 +393,9 @@
     def gathered(array, moves):
         pairs = []
         for d in range(0, dp_count, KEY_GROUPS):
-            for (group, chip), (source, home) in moves.items():
-                for core in range(2):
-                    start = (d + source) * ctx_count + home * 2 + core
-                    pairs.append((start, (d + group) * ctx_count + chip * 2 + core))
+            for (group, chip, core), (source, home) in moves.items():
+                start = (d + source) * ctx_count + home * 2 + core
+                pairs.append((start, (d + group) * ctx_count + chip * 2 + core))
         return lax.ppermute(array, ("dp", "ctx"), pairs)
 
     def spread(array, moves):
@@ -433,7 +432,8 @@
         for group in range(KEY_GROUPS):
             for chip in range(chips):
                 home = home_chip(spot, group, chip, chips)
-                ways = [k for k, moves in enumerate(rounds, 1) if moves.get((group, chip), (0, chip))[1] == home]
+                spot_key = (group, chip, 0)
+                ways = [k for k, m in enumerate(rounds, 1) if m.get(spot_key, (0, -1))[1] == home]
                 choices.append(0 if home == chip else ways[0] if home < chip else -1)
         used = sorted(set(choices) - {-1})
         (picked,) = call(
@@ -460,7 +460,11 @@
         + [((pair * width, rows), bf16)] * KEY_GROUPS,
         [query_v, grad_t, bias, blocks[-1], part_stats, part_sums],
         "attend",
-        scratch=[pltpu.VMEM((heads, rows), f32), pltpu.VMEM((width, rows), bf16)],
+        scratch=[
+            pltpu.VMEM((heads, rows), f32),
+            pltpu.VMEM((width, rows), bf16),
+            pltpu.VMEM((heads * width, rows), bf16),
+        ],
         work=1,
         dims=dims,
     )
@@ -525,18 +529,17 @@
         "join_heads",
         rounds=rounds,
     )
+    grad_q, pieces[-1] = call(
+        finish_query_kernel,
+        [((rows, pair * width), bf16), ((piece, 2 * width), bf16)],
+        all_dqs + pieces[-1:],
+        "finish_query",
+    )
     got = [spread(p, moves) for p, moves in zip(pieces, rounds)]
     for array in got[:-1]:
         (terms,) = call(add_kernel, [((piece, 2 * width), f32)], [terms, array], "add_terms")
-
-    grad_q, token = call(
-        finish_query_kernel,
-        [((rows, pair * width), bf16), ((8, 128), f32)],
-        all_dqs,
-        "finish_query",
-    )
     grad_k, grad_values = call(
-        finish_kernel, [((piece, width), bf16)] * 2, [token, terms, got[-1]], "finish"
+        finish_kernel, [((piece, width), bf16)] * 2, [terms, got[-1]], "finish"
     )
     return attn_out, grad_q, grad_k, grad_values
 

time: 37.9 us -> 38.3 us (1.011)
  waiting for transfers between devices: 8.41 us -> 11 us
  starting transfers between devices: 18.6 us -> 16.9 us
  Pallas kernels: 9.84 us -> 9.4 us
    ppermute x4 -> x3, waiting for transfers between devices: 0.13 us -> 2.75 us  [spread(): return lax.ppermute(array, 'ctx', pairs)]
    ppermute x4 -> x3, starting transfers between devices: 7.76 us -> 6.03 us  [spread(): return lax.ppermute(array, 'ctx', pairs)]
    pallas_call x17 -> x16, Pallas kernels: 9.84 us -> 9.4 us  [call(): pl.pallas_call(functools.partial(kernel, **static), out_shape=[jax.ShapeD...]
  transfers between devices with their start and end apart: 13 -> 12, of which waited for: 7 -> 7; matrix products, arithmetic and copies ran while one was open for 0% -> 0% of each run, Pallas kernels for 15% -> 15%
where the time goes in v1:
time: 38.3 us; the launch traced here: 38.1 us
  starting transfers between devices  16.9 us (44%)
  waiting for transfers between devices  11 us (29%)
  Pallas kernels  9.4 us (25%)
  between operations  0.79 us (2%)
    pallas_call x16, Pallas kernels, call(): pl.pallas_call(functools.partial(kernel, **static), out_shape=[jax.ShapeD...  9.4 us
    ppermute x2, starting transfers between devices, gathered(): return lax.ppermute(array, ('dp', 'ctx'), pairs)  8.25 us
    ppermute x3, starting transfers between devices, spread(): return lax.ppermute(array, 'ctx', pairs)  6.03 us
    ppermute x4, waiting for transfers between devices, over_dp(): return lax.ppermute(array, 'dp', [(d, d ^ flip) for d in range(dp_count)])  5.1 us
    ppermute x3, waiting for transfers between devices, spread(): return lax.ppermute(array, 'ctx', pairs)  2.75 us
    ppermute x4, starting transfers between devices, over_dp(): return lax.ppermute(array, 'dp', [(d, d ^ flip) for d in range(dp_count)])  2.37 us
    ppermute x3, waiting for transfers between devices, over_cores(): return lax.ppermute(array, 'ctx', [(c, c ^ 1) for c in range(ctx_count)])  1.58 us
    ppermute x2, waiting for transfers between devices, gathered(): return lax.ppermute(array, ('dp', 'ctx'), pairs)  1.58 us
  transfers between devices with their start and end apart: 12, of which 7 were waited for; matrix products, arithmetic and copies ran while one was open for 0% of the time, Pallas kernels for 15%

profile of v1, /device:TPU:0, one launch (start us, length us, event | category | flops | bytes accessed | tf_op | source)
XLA Modules:
  0.0 38.1 jit_solution(16702971004894734799)
XLA Ops:
  0.6 0.9 %load.1.refs_0_ = bf16[256,256]{1,0:T(8,128)(2,1)S(1)} custom-call(bf16[256,128]{1,0:T(8,128)(2,1)} %k_hbm.1, bf16[256,128]{1,0:T(8,128)(2,1)} %v_hbm.1), custom_call_target="tpu_custom_call" | custom-call | bytes 131072 | tf_op jit(solution)/shard_map/load/pallas_call | solution.py:367
  1.5 5.9 %collective-permute-start = (bf16[256,256]{1,0:T(8,128)(2,1)S(1)}, bf16[256,256]{1,0:T(8,128)(2,1)S(1)}, u32[]{:S(2)}, u32[]{:S(2)}) collective-permute-start(bf16[256,256]{1,0:T(8,128)(2,1)S(1)} %load.1.refs_0_), channel_id=1, source_target_pairs={{8,2},{0,4},{10,12},{4,6},{9,3},{1,5},{11,13},{13,7},{24,18},{16,2... | collective-permute-start | bytes 393224 | tf_op jit(solution)/shard_map/ppermute | solution.py:399
  7.5 2.3 %collective-permute-start.1 = (bf16[256,256]{1,0:T(8,128)(2,1)S(1)}, bf16[256,256]{1,0:T(8,128)(2,1)S(1)}, u32[]{:S(2)}, u32[]{:S(2)}) collective-permute-start(bf16[256,256]{1,0:T(8,128)(2,1)S(1)} %load.1.refs_0_), channel_id=1, source_target_pairs={{0,6},{10,14},{1,7},{11,15},{16,22},{26,30},{17,23},{27,31}} | collective-permute-start | bytes 393224 | tf_op jit(solution)/shard_map/ppermute | solution.py:399
  9.8 1.5 %prepare.1 = (bf16[256,512]{1,0:T(8,128)(2,1)S(1)}, bf16[256,512]{1,0:T(8,128)(2,1)S(1)}, bf16[512,256]{1,0:T(8,128)(2,1)S(1)}, f32[1024,256]{1,0:T(8,128)S(1)}, f32[8,128]{1,0:T(8,128)S(1)}) custom-call(s32[16,128]{1,0:T(8,128)} %bitcast.1, bf16[256,1024]{1,0:T(8,128)(2,1)} %q_hbm.1, bf16[256,1024]{1,0:T(8,128)(2,1)} %g_hbm.1), custom_call_target="tpu_custom_call" | custom-call | flops 268435456 | bytes 1312768 | tf_op jit(solution)/shard_map/prepare/pallas_call | solution.py:367
  11.3 0.0 collective-permute-done.refs_0_.refs_1_
  11.4 0.1 collective-permute-start.3
  11.4 1.6 %collective-permute-done.1.refs_1_ = bf16[256,256]{1,0:T(8,128)(2,1)S(1)} collective-permute-done((bf16[256,256]{1,0:T(8,128)(2,1)S(1)}, bf16[256,256]{1,0:T(8,128)(2,1)S(1)}, u32[]{:S(2)}, u32[]{:S(2)}) %collective-permute-start.1) | collective-permute-done | bytes 131104 | tf_op jit(solution)/shard_map/ppermute | solution.py:399
  13.0 0.1 collective-permute-start.2
  13.1 0.0 collective-permute-done.3.refs_1_
  13.1 1.2 %attend_most.1 = (f32[4,768,256]{2,1,0:T(8,128)S(1)}, f32[8,256]{1,0:T(8,128)S(1)}, f32[4,128,256]{2,1,0:T(8,128)S(1)}) custom-call(bf16[256,512]{1,0:T(8,128)(2,1)S(1)} %get-tuple-element.33.q_ref, f32[1024,256]{1,0:T(8,128)S(1)} %get-tuple-element.35.bias_ref, bf16[256,256]{1,0:T(8,128)(2,1)S(1)} %pick.3.refs_0_, ...), custom_call_target="tpu_custom_call" | custom-call | flops 536870912 | bytes 1839104 | tf_op jit(solution)/shard_map/attend_most/pallas_call | solution.py:367
  14.3 0.1 collective-permute-done.2.kv_ref.refs_3_
  14.5 0.7 %attend.1 = (f32[12,256]{1,0:T(8,128)S(1)}, f32[4,256,256]{2,1,0:T(8,128)S(1)}, bf16[256,256]{1,0:T(8,128)(2,1)S(1)}, bf16[256,256]{1,0:T(8,128)(2,1)S(1)}) custom-call(bf16[256,512]{1,0:T(8,128)(2,1)S(1)} %get-tuple-element.33.q_ref, bf16[512,256]{1,0:T(8,128)(2,1)S(1)} %get-tuple-element.34.gt_ref, f32[1024,256]{1,0:T(8,128)S(1)} %get-tuple-element.35.bias_ref, ...), custom_call_target="tpu_custom_call" | custom-call | flops 268435456 | bytes 792576 | tf_op jit(solution)/shard_map/attend/pallas_call | solution.py:367
  15.2 0.1 collective-permute-start.4
  15.2 0.7 %dprobs.1.refs_6_ = f32[4,1024,256]{2,1,0:T(8,128)S(1)} custom-call(bf16[256,512]{1,0:T(8,128)(2,1)S(1)} %get-tuple-element.43.g_ref, bf16[256,256]{1,0:T(8,128)(2,1)S(1)} %pick.3.refs_0_, bf16[256,256]{1,0:T(8,128)(2,1)S(1)} %collective-permute-done.3.refs_1_, bf16[256,256]{1,0:T(8,128)(2,1)S(1)} %pick.2.refs_2_, ...), custom_call_target="tpu_custom_call" | custom-call | flops 268435456 | bytes 2097152 | tf_op jit(solution)/shard_map/dprobs/pallas_call | solution.py:367
  16.0 3.0 %collective-permute-done.4.refs_1_.refs_8_ = f32[12,256]{1,0:T(8,128)S(1)} collective-permute-done((f32[12,256]{1,0:T(8,128)S(1)}, f32[12,256]{1,0:T(8,128)S(1)}, u32[]{:S(2)}, u32[]{:S(2)}) %collective-permute-start.4) | collective-permute-done | bytes 12320 | tf_op jit(solution)/shard_map/ppermute | solution.py:388
  19.0 1.6 %differentiate.1 = (bf16[4,1024,256]{2,1,0:T(8,128)(2,1)S(1)}, f32[512,256]{1,0:T(8,128)S(1)}, bf16[512,256]{1,0:T(8,128)(2,1)S(1)}) custom-call(bf16[256,512]{1,0:T(8,128)(2,1)S(1)} %get-tuple-element.33.q_ref, bf16[256,512]{1,0:T(8,128)(2,1)S(1)} %get-tuple-element.43.g_ref, bf16[256,256]{1,0:T(8,128)(2,1)S(1)} %pick.3.refs_0_, ...), custom_call_target="tpu_custom_call" | custom-call | flops 1073741824 | bytes 2621440 | tf_op jit(solution)/shard_map/differentiate/pallas_call | solution.py:367
  20.6 0.1 collective-permute-start.6
  20.7 0.1 collective-permute-start.5
  20.7 1.4 %collective-permute-done.6.got_ref = bf16[512,256]{1,0:T(8,128)(2,1)S(1)} collective-permute-done((bf16[512,256]{1,0:T(8,128)(2,1)S(1)}, bf16[512,256]{1,0:T(8,128)(2,1)S(1)}, u32[]{:S(2)}, u32[]{:S(2)}) %collective-permute-start.6) | collective-permute-done | bytes 262176 | tf_op jit(solution)/shard_map/ppermute | solution.py:391
  22.2 1.6 %collective-permute-start.8 = (bf16[256,256]{1,0:T(8,128)(2,1)S(1)}, bf16[256,256]{1,0:T(8,128)(2,1)S(1)}, u32[]{:S(2)}, u32[]{:S(2)}) collective-permute-start(bf16[256,256]{1,0:T(8,128)(2,1)S(1)} %get-tuple-element.52), channel_id=1, source_target_pairs={{0,16},{8,24},{16,0},{24,8},{1,17},{9,25},{17,1},{25,9},{2,18},{10... | collective-permute-start | bytes 393224 | tf_op jit(solution)/shard_map/ppermute | solution.py:388
  23.8 0.5 %query_terms.1 = (bf16[256,256]{1,0:T(8,128)(2,1)S(1)}, bf16[256,256]{1,0:T(8,128)(2,1)S(1)}) custom-call(bf16[256,256]{1,0:T(8,128)(2,1)S(1)} %pick.3.refs_0_, bf16[256,256]{1,0:T(8,128)(2,1)S(1)} %collective-permute-done.3.refs_1_, bf16[256,256]{1,0:T(8,128)(2,1)S(1)} %pick.2.refs_2_, bf16[256,256]{1,0:T(8,128)(2,1)S(1)} %collective-permute-done.2.kv_ref.refs_3_, ...), custom_call_target="tpu_custom_call" | custom-call | flops 268435456 | bytes 262144 | tf_op jit(solution)/shard_map/query_terms/pallas_call | solution.py:367
  24.3 0.6 %collective-permute-start.7 = (bf16[256,256]{1,0:T(8,128)(2,1)S(1)}, bf16[256,256]{1,0:T(8,128)(2,1)S(1)}, u32[]{:S(2)}, u32[]{:S(2)}) collective-permute-start(bf16[256,256]{1,0:T(8,128)(2,1)S(1)} %get-tuple-element.51), channel_id=1, source_target_pairs={{0,8},{8,0},{16,24},{24,16},{1,9},{9,1},{17,25},{25,17},{2,10},{10... | collective-permute-start | bytes 393224 | tf_op jit(solution)/shard_map/ppermute | solution.py:388
  24.9 1.6 %collective-permute-done.5.refs_3_ = bf16[256,256]{1,0:T(8,128)(2,1)S(1)} collective-permute-done((bf16[256,256]{1,0:T(8,128)(2,1)S(1)}, bf16[256,256]{1,0:T(8,128)(2,1)S(1)}, u32[]{:S(2)}, u32[]{:S(2)}) %collective-permute-start.5) | collective-permute-done | bytes 131104 | tf_op jit(solution)/shard_map/ppermute | solution.py:388
  26.6 0.8 %finish_out.1 = (bf16[256,256]{1,0:T(8,128)(2,1)}, f32[8,128]{1,0:T(8,128)S(1)}) custom-call(f32[12,256]{1,0:T(8,128)S(1)} %get-tuple-element.39.refs_0_.refs_7_, f32[12,256]{1,0:T(8,128)S(1)} %collective-permute-done.4.refs_1_.refs_8_, bf16[256,256]{1,0:T(8,128)(2,1)S(1)} %get-tuple-element.40.refs_2_, bf16[256,256]{1,0:T(8,128)(2,1)S(1)} %collective-permute-done.5.refs_3_), custom_call_target="tpu_custom_call" | custom-call | bytes 133120 | tf_op jit(solution)/shard_map/finish_out/pallas_call | solution.py:367
  27.4 0.4 %collective-permute-done.8.got_ref = bf16[256,256]{1,0:T(8,128)(2,1)S(1)} collective-permute-done((bf16[256,256]{1,0:T(8,128)(2,1)S(1)}, bf16[256,256]{1,0:T(8,128)(2,1)S(1)}, u32[]{:S(2)}, u32[]{:S(2)}) %collective-permute-start.8) | collective-permute-done | bytes 131104 | tf_op jit(solution)/shard_map/ppermute | solution.py:388
  27.9 0.8 %collective-permute-start.9 = (bf16[64,256]{1,0:T(8,128)(2,1)S(1)}, bf16[64,256]{1,0:T(8,128)(2,1)S(1)}, u32[]{:S(2)}, u32[]{:S(2)}) collective-permute-start(bf16[64,256]{1,0:T(8,128)(2,1)S(1)} %get-tuple-element.57), channel_id=1, source_target_pairs={{0,2},{1,3},{2,4},{3,5},{4,6},{5,7},{6,0},{7,1},{8,10},{9,11},{10,... | collective-permute-start | bytes 98312 | tf_op jit(solution)/shard_map/ppermute | solution.py:403
  28.7 4.1 %collective-permute-start.10 = (bf16[64,256]{1,0:T(8,128)(2,1)S(1)}, bf16[64,256]{1,0:T(8,128)(2,1)S(1)}, u32[]{:S(2)}, u32[]{:S(2)}) collective-permute-start(bf16[64,256]{1,0:T(8,128)(2,1)S(1)} %get-tuple-element.58), channel_id=1, source_target_pairs={{0,4},{1,5},{2,6},{3,7},{4,0},{5,1},{6,2},{7,3},{8,12},{9,13},{10,... | collective-permute-start | bytes 98312 | tf_op jit(solution)/shard_map/ppermute | solution.py:403
  32.8 0.0 collective-permute-done.7.got_ref
  32.8 0.8 %finish_query.1 = (bf16[256,256]{1,0:T(8,128)(2,1)}, bf16[64,256]{1,0:T(8,128)(2,1)S(1)}) custom-call(bf16[256,256]{1,0:T(8,128)(2,1)S(1)} %get-tuple-element.50.own_ref, bf16[256,256]{1,0:T(8,128)(2,1)S(1)} %collective-permute-done.7.got_ref, bf16[64,256]{1,0:T(8,128)(2,1)S(1)} %get-tuple-element.54.piece_ref), custom_call_target="tpu_custom_call" | custom-call | bytes 163840 | tf_op jit(solution)/shard_map/finish_query/pallas_call | solution.py:367
  33.5 1.1 %collective-permute-start.11 = (bf16[64,256]{1,0:T(8,128)(2,1)S(1)}, bf16[64,256]{1,0:T(8,128)(2,1)S(1)}, u32[]{:S(2)}, u32[]{:S(2)}) collective-permute-start(bf16[64,256]{1,0:T(8,128)(2,1)S(1)} %get-tuple-element.59), channel_id=1, source_target_pairs={{0,6},{1,7},{2,0},{3,1},{4,2},{5,3},{6,4},{7,5},{8,14},{9,15},{10,... | collective-permute-start | bytes 98312 | tf_op jit(solution)/shard_map/ppermute | solution.py:403
  34.7 0.0 collective-permute-done.9.second_ref
  34.7 0.0 collective-permute-done.10.second_ref
  34.7 2.7 %collective-permute-done.11.refs_1_ = bf16[64,256]{1,0:T(8,128)(2,1)S(1)} collective-permute-done((bf16[64,256]{1,0:T(8,128)(2,1)S(1)}, bf16[64,256]{1,0:T(8,128)(2,1)S(1)}, u32[]{:S(2)}, u32[]{:S(2)}) %collective-permute-start.11) | collective-permute-done | bytes 32800 | tf_op jit(solution)/shard_map/ppermute | solution.py:403
  37.4 0.6 %finish.1 = (bf16[64,128]{1,0:T(8,128)(2,1)}, bf16[64,128]{1,0:T(8,128)(2,1)}) custom-call(f32[64,256]{1,0:T(8,128)S(1)} %add_terms.3.refs_0_, bf16[64,256]{1,0:T(8,128)(2,1)S(1)} %collective-permute-done.11.refs_1_), custom_call_target="tpu_custom_call" | custom-call | bytes 32768 | tf_op jit(solution)/shard_map/finish/pallas_call | solution.py:367
  (6 shorter events, 0.2 us)
Async XLA Ops:
  1.5 9.8 %collective-permute-start = (bf16[256,256]{1,0:T(8,128)(2,1)S(1)}, bf16[256,256]{1,0:T(8,128)(2,1)S(1)}, u32[]{:S(2)}, u32[]{:S(2)}) collective-permute-start(bf16[256,256]{1,0:T(8,128)(2,1)S(1)} %load.1.refs_0_), channel_id=1, source_target_pairs={{8,2},{0,4},{10,12},{4,6},{9,3},{1,5},{11,13},{13,7},{24,18},{16,2... | collective-permute-start | bytes 393224 | tf_op jit(solution)/shard_map/ppermute | solution.py:399
  7.5 5.5 %collective-permute-start.1 = (bf16[256,256]{1,0:T(8,128)(2,1)S(1)}, bf16[256,256]{1,0:T(8,128)(2,1)S(1)}, u32[]{:S(2)}, u32[]{:S(2)}) collective-permute-start(bf16[256,256]{1,0:T(8,128)(2,1)S(1)} %load.1.refs_0_), channel_id=1, source_target_pairs={{0,6},{10,14},{1,7},{11,15},{16,22},{26,30},{17,23},{27,31}} | collective-permute-start | bytes 393224 | tf_op jit(solution)/shard_map/ppermute | solution.py:399
  11.4 1.8 %collective-permute-start.3 = (bf16[256,256]{1,0:T(8,128)(2,1)S(1)}, bf16[256,256]{1,0:T(8,128)(2,1)S(1)}, u32[]{:S(2)}, u32[]{:S(2)}) collective-permute-start(bf16[256,256]{1,0:T(8,128)(2,1)S(1)} %pick.3.refs_0_), channel_id=1, source_target_pairs={{0,1},{1,0},{2,3},{3,2},{4,5},{5,4},{6,7},{7,6},{8,9},{9,8},{10,11... | collective-permute-start | bytes 393224 | tf_op jit(solution)/shard_map/ppermute | solution.py:391
  13.0 1.4 %collective-permute-start.2 = (bf16[256,256]{1,0:T(8,128)(2,1)S(1)}, bf16[256,256]{1,0:T(8,128)(2,1)S(1)}, u32[]{:S(2)}, u32[]{:S(2)}) collective-permute-start(bf16[256,256]{1,0:T(8,128)(2,1)S(1)} %pick.2.refs_2_), channel_id=1, source_target_pairs={{0,1},{1,0},{2,3},{3,2},{4,5},{5,4},{6,7},{7,6},{8,9},{9,8},{10,11... | collective-permute-start | bytes 393224 | tf_op jit(solution)/shard_map/ppermute | solution.py:391
  15.2 3.8 %collective-permute-start.4 = (f32[12,256]{1,0:T(8,128)S(1)}, f32[12,256]{1,0:T(8,128)S(1)}, u32[]{:S(2)}, u32[]{:S(2)}) collective-permute-start(f32[12,256]{1,0:T(8,128)S(1)} %get-tuple-element.39.refs_0_.refs_7_), channel_id=1, source_target_pairs={{0,8},{8,0},{16,24},{24,16},{1,9},{9,1},{17,25},{25,17},{2,10},{10... | collective-permute-start | bytes 36872 | tf_op jit(solution)/shard_map/ppermute | solution.py:388
  20.6 1.6 %collective-permute-start.6 = (bf16[512,256]{1,0:T(8,128)(2,1)S(1)}, bf16[512,256]{1,0:T(8,128)(2,1)S(1)}, u32[]{:S(2)}, u32[]{:S(2)}) collective-permute-start(bf16[512,256]{1,0:T(8,128)(2,1)S(1)} %get-tuple-element.48), channel_id=1, source_target_pairs={{0,1},{1,0},{2,3},{3,2},{4,5},{5,4},{6,7},{7,6},{8,9},{9,8},{10,11... | collective-permute-start | bytes 786440 | tf_op jit(solution)/shard_map/ppermute | solution.py:391
  20.7 5.9 %collective-permute-start.5 = (bf16[256,256]{1,0:T(8,128)(2,1)S(1)}, bf16[256,256]{1,0:T(8,128)(2,1)S(1)}, u32[]{:S(2)}, u32[]{:S(2)}) collective-permute-start(bf16[256,256]{1,0:T(8,128)(2,1)S(1)} %get-tuple-element.41), channel_id=1, source_target_pairs={{0,8},{8,0},{16,24},{24,16},{1,9},{9,1},{17,25},{25,17},{2,10},{10... | collective-permute-start | bytes 393224 | tf_op jit(solution)/shard_map/ppermute | solution.py:388
  22.2 5.6 %collective-permute-start.8 = (bf16[256,256]{1,0:T(8,128)(2,1)S(1)}, bf16[256,256]{1,0:T(8,128)(2,1)S(1)}, u32[]{:S(2)}, u32[]{:S(2)}) collective-permute-start(bf16[256,256]{1,0:T(8,128)(2,1)S(1)} %get-tuple-element.52), channel_id=1, source_target_pairs={{0,16},{8,24},{16,0},{24,8},{1,17},{9,25},{17,1},{25,9},{2,18},{10... | collective-permute-start | bytes 393224 | tf_op jit(solution)/shard_map/ppermute | solution.py:388
  24.3 8.5 %collective-permute-start.7 = (bf16[256,256]{1,0:T(8,128)(2,1)S(1)}, bf16[256,256]{1,0:T(8,128)(2,1)S(1)}, u32[]{:S(2)}, u32[]{:S(2)}) collective-permute-start(bf16[256,256]{1,0:T(8,128)(2,1)S(1)} %get-tuple-element.51), channel_id=1, source_target_pairs={{0,8},{8,0},{16,24},{24,16},{1,9},{9,1},{17,25},{25,17},{2,10},{10... | collective-permute-start | bytes 393224 | tf_op jit(solution)/shard_map/ppermute | solution.py:388
  27.9 6.8 %collective-permute-start.9 = (bf16[64,256]{1,0:T(8,128)(2,1)S(1)}, bf16[64,256]{1,0:T(8,128)(2,1)S(1)}, u32[]{:S(2)}, u32[]{:S(2)}) collective-permute-start(bf16[64,256]{1,0:T(8,128)(2,1)S(1)} %get-tuple-element.57), channel_id=1, source_target_pairs={{0,2},{1,3},{2,4},{3,5},{4,6},{5,7},{6,0},{7,1},{8,10},{9,11},{10,... | collective-permute-start | bytes 98312 | tf_op jit(solution)/shard_map/ppermute | solution.py:403
  28.7 6.1 %collective-permute-start.10 = (bf16[64,256]{1,0:T(8,128)(2,1)S(1)}, bf16[64,256]{1,0:T(8,128)(2,1)S(1)}, u32[]{:S(2)}, u32[]{:S(2)}) collective-permute-start(bf16[64,256]{1,0:T(8,128)(2,1)S(1)} %get-tuple-element.58), channel_id=1, source_target_pairs={{0,4},{1,5},{2,6},{3,7},{4,0},{5,1},{6,2},{7,3},{8,12},{9,13},{10,... | collective-permute-start | bytes 98312 | tf_op jit(solution)/shard_map/ppermute | solution.py:403
  33.5 3.9 %collective-permute-start.11 = (bf16[64,256]{1,0:T(8,128)(2,1)S(1)}, bf16[64,256]{1,0:T(8,128)(2,1)S(1)}, u32[]{:S(2)}, u32[]{:S(2)}) collective-permute-start(bf16[64,256]{1,0:T(8,128)(2,1)S(1)} %get-tuple-element.59), channel_id=1, source_target_pairs={{0,6},{1,7},{2,0},{3,1},{4,2},{5,3},{6,4},{7,5},{8,14},{9,15},{10,... | collective-permute-start | bytes 98312 | tf_op jit(solution)/shard_map/ppermute | solution.py:403

commit v2 on v1

--- a/solution.py
+++ b/solution.py
@@ -49,6 +49,8 @@
 
 
 def spread_rounds(chips):
+    if chips == 4:
+        return [{3: 0, 0: 1, 1: 2}, {2: 0, 3: 1, 0: 2, 1: 3}, {1: 0, 2: 1, 3: 2, 0: 3}, {2: 3}]
     return [{chip: (chip + step) % chips for chip in range(chips)} for step in range(1, chips)]
 
 
@@ -328,13 +330,13 @@
         attn_ref[:, here] = (joined / pick(total)).T.astype(jnp.bfloat16)
 
 
-def finish_query_kernel(own_ref, got_ref, piece_ref, gq_ref, passed_ref):
+def finish_query_kernel(own_ref, got_ref, gq_ref, token_ref):
     total = own_ref[...].astype(jnp.float32) + got_ref[...].astype(jnp.float32)
     gq_ref[...] = total.T.astype(jnp.bfloat16)
-    passed_ref[...] = piece_ref[...]
-
-
-def finish_kernel(*refs):
+    token_ref[...] = jnp.zeros_like(token_ref)
+
+
+def finish_kernel(token_ref, *refs):
     *terms, gk_ref, gv_ref = refs
     width = gk_ref.shape[1]
     both = sum(r[...].astype(jnp.float32) for r in terms)
@@ -529,17 +531,17 @@
         "join_heads",
         rounds=rounds,
     )
-    grad_q, pieces[-1] = call(
+    grad_q, token = call(
         finish_query_kernel,
-        [((rows, pair * width), bf16), ((piece, 2 * width), bf16)],
-        all_dqs + pieces[-1:],
+        [((rows, pair * width), bf16), ((8, 128), f32)],
+        all_dqs,
         "finish_query",
     )
     got = [spread(p, moves) for p, moves in zip(pieces, rounds)]
     for array in got[:-1]:
         (terms,) = call(add_kernel, [((piece, 2 * width), f32)], [terms, array], "add_terms")
     grad_k, grad_values = call(
-        finish_kernel, [((piece, width), bf16)] * 2, [terms, got[-1]], "finish"
+        finish_kernel, [((piece, width), bf16)] * 2, [token, terms, got[-1]], "finish"
     )
     return attn_out, grad_q, grad_k, grad_values
 

time: 38.3 us -> 37.5 us (0.979)
  waiting for transfers between devices: 11 us -> 8.38 us
  starting transfers between devices: 16.9 us -> 18.6 us
    ppermute x3 -> x4, waiting for transfers between devices: 2.75 us -> 0.13 us  [spread(): return lax.ppermute(array, 'ctx', pairs)]
    ppermute x3 -> x4, starting transfers between devices: 6.03 us -> 7.76 us  [spread(): return lax.ppermute(array, 'ctx', pairs)]
    pallas_call x16 -> x17, Pallas kernels: 9.4 us -> 9.42 us  [call(): pl.pallas_call(functools.partial(kernel, **static), out_shape=[jax.ShapeD...]
  transfers between devices with their start and end apart: 12 -> 13, of which waited for: 7 -> 7; matrix products, arithmetic and copies ran while one was open for 0% -> 0% of each run, Pallas kernels for 15% -> 15%
where the time goes in v2:
time: 37.5 us; the launch traced here: 37.2 us
  starting transfers between devices  18.6 us (50%)
  Pallas kernels  9.42 us (25%)
  waiting for transfers between devices  8.38 us (22%)
  between operations  0.83 us (2%)
    pallas_call x17, Pallas kernels, call(): pl.pallas_call(functools.partial(kernel, **static), out_shape=[jax.ShapeD...  9.42 us
    ppermute x2, starting transfers between devices, gathered(): return lax.ppermute(array, ('dp', 'ctx'), pairs)  8.25 us
    ppermute x4, starting transfers between devices, spread(): return lax.ppermute(array, 'ctx', pairs)  7.76 us
    ppermute x4, waiting for transfers between devices, over_dp(): return lax.ppermute(array, 'dp', [(d, d ^ flip) for d in range(dp_count)])  5.09 us
    ppermute x4, starting transfers between devices, over_dp(): return lax.ppermute(array, 'dp', [(d, d ^ flip) for d in range(dp_count)])  2.37 us
    ppermute x3, waiting for transfers between devices, over_cores(): return lax.ppermute(array, 'ctx', [(c, c ^ 1) for c in range(ctx_count)])  1.58 us
    ppermute x2, waiting for transfers between devices, gathered(): return lax.ppermute(array, ('dp', 'ctx'), pairs)  1.58 us
  transfers between devices with their start and end apart: 13, of which 7 were waited for; matrix products, arithmetic and copies ran while one was open for 0% of the time, Pallas kernels for 15%

profile of v2, /device:TPU:0, one launch (start us, length us, event | category | flops | bytes accessed | tf_op | source)
XLA Modules:
  0.0 37.2 jit_solution(9308015186818529609)
XLA Ops:
  0.6 0.9 %load.1.refs_0_ = bf16[256,256]{1,0:T(8,128)(2,1)S(1)} custom-call(bf16[256,128]{1,0:T(8,128)(2,1)} %k_hbm.1, bf16[256,128]{1,0:T(8,128)(2,1)} %v_hbm.1), custom_call_target="tpu_custom_call" | custom-call | bytes 131072 | tf_op jit(solution)/shard_map/load/pallas_call | solution.py:369
  1.5 5.9 %collective-permute-start = (bf16[256,256]{1,0:T(8,128)(2,1)S(1)}, bf16[256,256]{1,0:T(8,128)(2,1)S(1)}, u32[]{:S(2)}, u32[]{:S(2)}) collective-permute-start(bf16[256,256]{1,0:T(8,128)(2,1)S(1)} %load.1.refs_0_), channel_id=1, source_target_pairs={{8,2},{0,4},{10,12},{4,6},{9,3},{1,5},{11,13},{13,7},{24,18},{16,2... | collective-permute-start | bytes 393224 | tf_op jit(solution)/shard_map/ppermute | solution.py:401
  7.5 2.3 %collective-permute-start.1 = (bf16[256,256]{1,0:T(8,128)(2,1)S(1)}, bf16[256,256]{1,0:T(8,128)(2,1)S(1)}, u32[]{:S(2)}, u32[]{:S(2)}) collective-permute-start(bf16[256,256]{1,0:T(8,128)(2,1)S(1)} %load.1.refs_0_), channel_id=1, source_target_pairs={{0,6},{10,14},{1,7},{11,15},{16,22},{26,30},{17,23},{27,31}} | collective-permute-start | bytes 393224 | tf_op jit(solution)/shard_map/ppermute | solution.py:401
  9.8 1.5 %prepare.1 = (bf16[256,512]{1,0:T(8,128)(2,1)S(1)}, bf16[256,512]{1,0:T(8,128)(2,1)S(1)}, bf16[512,256]{1,0:T(8,128)(2,1)S(1)}, f32[1024,256]{1,0:T(8,128)S(1)}, f32[8,128]{1,0:T(8,128)S(1)}) custom-call(s32[16,128]{1,0:T(8,128)} %bitcast.1, bf16[256,1024]{1,0:T(8,128)(2,1)} %q_hbm.1, bf16[256,1024]{1,0:T(8,128)(2,1)} %g_hbm.1), custom_call_target="tpu_custom_call" | custom-call | flops 268435456 | bytes 1312768 | tf_op jit(solution)/shard_map/prepare/pallas_call | solution.py:369
  11.3 0.0 collective-permute-done.refs_0_.refs_1_
  11.4 0.1 collective-permute-start.3
  11.4 1.6 %collective-permute-done.1.refs_1_ = bf16[256,256]{1,0:T(8,128)(2,1)S(1)} collective-permute-done((bf16[256,256]{1,0:T(8,128)(2,1)S(1)}, bf16[256,256]{1,0:T(8,128)(2,1)S(1)}, u32[]{:S(2)}, u32[]{:S(2)}) %collective-permute-start.1) | collective-permute-done | bytes 131104 | tf_op jit(solution)/shard_map/ppermute | solution.py:401
  13.0 0.1 collective-permute-start.2
  13.1 0.0 collective-permute-done.3.refs_1_
  13.1 1.2 %attend_most.1 = (f32[4,768,256]{2,1,0:T(8,128)S(1)}, f32[8,256]{1,0:T(8,128)S(1)}, f32[4,128,256]{2,1,0:T(8,128)S(1)}) custom-call(bf16[256,512]{1,0:T(8,128)(2,1)S(1)} %get-tuple-element.34.q_ref, f32[1024,256]{1,0:T(8,128)S(1)} %get-tuple-element.36.bias_ref, bf16[256,256]{1,0:T(8,128)(2,1)S(1)} %pick.3.refs_0_, ...), custom_call_target="tpu_custom_call" | custom-call | flops 536870912 | bytes 1839104 | tf_op jit(solution)/shard_map/attend_most/pallas_call | solution.py:369
  14.3 0.1 collective-permute-done.2.kv_ref.refs_3_
  14.5 0.7 %attend.1 = (f32[12,256]{1,0:T(8,128)S(1)}, f32[4,256,256]{2,1,0:T(8,128)S(1)}, bf16[256,256]{1,0:T(8,128)(2,1)S(1)}, bf16[256,256]{1,0:T(8,128)(2,1)S(1)}) custom-call(bf16[256,512]{1,0:T(8,128)(2,1)S(1)} %get-tuple-element.34.q_ref, bf16[512,256]{1,0:T(8,128)(2,1)S(1)} %get-tuple-element.35.gt_ref, f32[1024,256]{1,0:T(8,128)S(1)} %get-tuple-element.36.bias_ref, ...), custom_call_target="tpu_custom_call" | custom-call | flops 268435456 | bytes 792576 | tf_op jit(solution)/shard_map/attend/pallas_call | solution.py:369
  15.2 0.1 collective-permute-start.4
  15.2 0.7 %dprobs.1.refs_6_ = f32[4,1024,256]{2,1,0:T(8,128)S(1)} custom-call(bf16[256,512]{1,0:T(8,128)(2,1)S(1)} %get-tuple-element.44.g_ref, bf16[256,256]{1,0:T(8,128)(2,1)S(1)} %pick.3.refs_0_, bf16[256,256]{1,0:T(8,128)(2,1)S(1)} %collective-permute-done.3.refs_1_, bf16[256,256]{1,0:T(8,128)(2,1)S(1)} %pick.2.refs_2_, ...), custom_call_target="tpu_custom_call" | custom-call | flops 268435456 | bytes 2097152 | tf_op jit(solution)/shard_map/dprobs/pallas_call | solution.py:369
  16.0 3.0 %collective-permute-done.4.refs_1_.refs_8_ = f32[12,256]{1,0:T(8,128)S(1)} collective-permute-done((f32[12,256]{1,0:T(8,128)S(1)}, f32[12,256]{1,0:T(8,128)S(1)}, u32[]{:S(2)}, u32[]{:S(2)}) %collective-permute-start.4) | collective-permute-done | bytes 12320 | tf_op jit(solution)/shard_map/ppermute | solution.py:390
  19.0 1.6 %differentiate.1 = (bf16[4,1024,256]{2,1,0:T(8,128)(2,1)S(1)}, f32[512,256]{1,0:T(8,128)S(1)}, bf16[512,256]{1,0:T(8,128)(2,1)S(1)}) custom-call(bf16[256,512]{1,0:T(8,128)(2,1)S(1)} %get-tuple-element.34.q_ref, bf16[256,512]{1,0:T(8,128)(2,1)S(1)} %get-tuple-element.44.g_ref, bf16[256,256]{1,0:T(8,128)(2,1)S(1)} %pick.3.refs_0_, ...), custom_call_target="tpu_custom_call" | custom-call | flops 1073741824 | bytes 2621440 | tf_op jit(solution)/shard_map/differentiate/pallas_call | solution.py:369
  20.6 0.1 collective-permute-start.6
  20.7 0.1 collective-permute-start.5
  20.7 1.4 %collective-permute-done.6.got_ref = bf16[512,256]{1,0:T(8,128)(2,1)S(1)} collective-permute-done((bf16[512,256]{1,0:T(8,128)(2,1)S(1)}, bf16[512,256]{1,0:T(8,128)(2,1)S(1)}, u32[]{:S(2)}, u32[]{:S(2)}) %collective-permute-start.6) | collective-permute-done | bytes 262176 | tf_op jit(solution)/shard_map/ppermute | solution.py:393
  22.2 1.6 %collective-permute-start.8 = (bf16[256,256]{1,0:T(8,128)(2,1)S(1)}, bf16[256,256]{1,0:T(8,128)(2,1)S(1)}, u32[]{:S(2)}, u32[]{:S(2)}) collective-permute-start(bf16[256,256]{1,0:T(8,128)(2,1)S(1)} %get-tuple-element.55), channel_id=1, source_target_pairs={{0,16},{8,24},{16,0},{24,8},{1,17},{9,25},{17,1},{25,9},{2,18},{10... | collective-permute-start | bytes 393224 | tf_op jit(solution)/shard_map/ppermute | solution.py:390
  23.8 0.5 %query_terms.1 = (bf16[256,256]{1,0:T(8,128)(2,1)S(1)}, bf16[256,256]{1,0:T(8,128)(2,1)S(1)}) custom-call(bf16[256,256]{1,0:T(8,128)(2,1)S(1)} %pick.3.refs_0_, bf16[256,256]{1,0:T(8,128)(2,1)S(1)} %collective-permute-done.3.refs_1_, bf16[256,256]{1,0:T(8,128)(2,1)S(1)} %pick.2.refs_2_, bf16[256,256]{1,0:T(8,128)(2,1)S(1)} %collective-permute-done.2.kv_ref.refs_3_, ...), custom_call_target="tpu_custom_call" | custom-call | flops 268435456 | bytes 262144 | tf_op jit(solution)/shard_map/query_terms/pallas_call | solution.py:369
  24.3 0.6 %collective-permute-start.7 = (bf16[256,256]{1,0:T(8,128)(2,1)S(1)}, bf16[256,256]{1,0:T(8,128)(2,1)S(1)}, u32[]{:S(2)}, u32[]{:S(2)}) collective-permute-start(bf16[256,256]{1,0:T(8,128)(2,1)S(1)} %get-tuple-element.52), channel_id=1, source_target_pairs={{0,8},{8,0},{16,24},{24,16},{1,9},{9,1},{17,25},{25,17},{2,10},{10... | collective-permute-start | bytes 393224 | tf_op jit(solution)/shard_map/ppermute | solution.py:390
  24.9 1.6 %collective-permute-done.5.refs_3_ = bf16[256,256]{1,0:T(8,128)(2,1)S(1)} collective-permute-done((bf16[256,256]{1,0:T(8,128)(2,1)S(1)}, bf16[256,256]{1,0:T(8,128)(2,1)S(1)}, u32[]{:S(2)}, u32[]{:S(2)}) %collective-permute-start.5) | collective-permute-done | bytes 131104 | tf_op jit(solution)/shard_map/ppermute | solution.py:390
  26.6 0.8 %finish_out.1 = (bf16[256,256]{1,0:T(8,128)(2,1)}, f32[8,128]{1,0:T(8,128)S(1)}) custom-call(f32[12,256]{1,0:T(8,128)S(1)} %get-tuple-element.40.refs_0_.refs_7_, f32[12,256]{1,0:T(8,128)S(1)} %collective-permute-done.4.refs_1_.refs_8_, bf16[256,256]{1,0:T(8,128)(2,1)S(1)} %get-tuple-element.41.refs_2_, bf16[256,256]{1,0:T(8,128)(2,1)S(1)} %collective-permute-done.5.refs_3_), custom_call_target="tpu_custom_call" | custom-call | bytes 133120 | tf_op jit(solution)/shard_map/finish_out/pallas_call | solution.py:369
  27.4 0.4 %collective-permute-done.8.got_ref = bf16[256,256]{1,0:T(8,128)(2,1)S(1)} collective-permute-done((bf16[256,256]{1,0:T(8,128)(2,1)S(1)}, bf16[256,256]{1,0:T(8,128)(2,1)S(1)}, u32[]{:S(2)}, u32[]{:S(2)}) %collective-permute-start.8) | collective-permute-done | bytes 131104 | tf_op jit(solution)/shard_map/ppermute | solution.py:390
  27.9 2.6 %collective-permute-start.9 = (bf16[64,256]{1,0:T(8,128)(2,1)S(1)}, bf16[64,256]{1,0:T(8,128)(2,1)S(1)}, u32[]{:S(2)}, u32[]{:S(2)}) collective-permute-start(bf16[64,256]{1,0:T(8,128)(2,1)S(1)} %get-tuple-element.58), channel_id=1, source_target_pairs={{6,0},{7,1},{0,2},{1,3},{2,4},{3,5},{14,8},{15,9},{8,10},{9,11},{1... | collective-permute-start | bytes 98312 | tf_op jit(solution)/shard_map/ppermute | solution.py:405
  30.5 0.9 %collective-permute-start.10 = (bf16[64,256]{1,0:T(8,128)(2,1)S(1)}, bf16[64,256]{1,0:T(8,128)(2,1)S(1)}, u32[]{:S(2)}, u32[]{:S(2)}) collective-permute-start(bf16[64,256]{1,0:T(8,128)(2,1)S(1)} %get-tuple-element.59), channel_id=1, source_target_pairs={{4,0},{5,1},{6,2},{7,3},{0,4},{1,5},{2,6},{3,7},{12,8},{13,9},{14,... | collective-permute-start | bytes 98312 | tf_op jit(solution)/shard_map/ppermute | solution.py:405
  31.5 3.5 %collective-permute-start.11 = (bf16[64,256]{1,0:T(8,128)(2,1)S(1)}, bf16[64,256]{1,0:T(8,128)(2,1)S(1)}, u32[]{:S(2)}, u32[]{:S(2)}) collective-permute-start(bf16[64,256]{1,0:T(8,128)(2,1)S(1)} %get-tuple-element.60), channel_id=1, source_target_pairs={{2,0},{3,1},{4,2},{5,3},{6,4},{7,5},{0,6},{1,7},{10,8},{11,9},{12,... | collective-permute-start | bytes 98312 | tf_op jit(solution)/shard_map/ppermute | solution.py:405
  35.0 0.7 %collective-permute-start.12 = (bf16[64,256]{1,0:T(8,128)(2,1)S(1)}, bf16[64,256]{1,0:T(8,128)(2,1)S(1)}, u32[]{:S(2)}, u32[]{:S(2)}) collective-permute-start(bf16[64,256]{1,0:T(8,128)(2,1)S(1)} %get-tuple-element.61), channel_id=1, source_target_pairs={{4,6},{5,7},{12,14},{13,15},{20,22},{21,23},{28,30},{29,31}} | collective-permute-start | bytes 98312 | tf_op jit(solution)/shard_map/ppermute | solution.py:405
  35.7 0.0 collective-permute-done.7.got_ref
  35.7 0.8 %finish_query.1 = (bf16[256,256]{1,0:T(8,128)(2,1)}, f32[8,128]{1,0:T(8,128)S(1)}) custom-call(bf16[256,256]{1,0:T(8,128)(2,1)S(1)} %get-tuple-element.51.own_ref, bf16[256,256]{1,0:T(8,128)(2,1)S(1)} %collective-permute-done.7.got_ref), custom_call_target="tpu_custom_call" | custom-call | bytes 133120 | tf_op jit(solution)/shard_map/finish_query/pallas_call | solution.py:369
  36.4 0.0 collective-permute-done.9.second_ref
  36.4 0.0 collective-permute-done.10.second_ref
  36.5 0.1 collective-permute-done.11.second_ref
  36.6 0.0 collective-permute-done.12.refs_1_
  36.6 0.6 %finish.1 = (bf16[64,128]{1,0:T(8,128)(2,1)}, bf16[64,128]{1,0:T(8,128)(2,1)}) custom-call(f32[8,128]{1,0:T(8,128)S(1)} %get-tuple-element.54.token_ref, f32[64,256]{1,0:T(8,128)S(1)} %add_terms.5.refs_0_, bf16[64,256]{1,0:T(8,128)(2,1)S(1)} %collective-permute-done.12.refs_1_), custom_call_target="tpu_custom_call" | custom-call | bytes 32768 | tf_op jit(solution)/shard_map/finish/pallas_call | solution.py:369
  (7 shorter events, 0.2 us)
Async XLA Ops:
  1.5 9.8 %collective-permute-start = (bf16[256,256]{1,0:T(8,128)(2,1)S(1)}, bf16[256,256]{1,0:T(8,128)(2,1)S(1)}, u32[]{:S(2)}, u32[]{:S(2)}) collective-permute-start(bf16[256,256]{1,0:T(8,128)(2,1)S(1)} %load.1.refs_0_), channel_id=1, source_target_pairs={{8,2},{0,4},{10,12},{4,6},{9,3},{1,5},{11,13},{13,7},{24,18},{16,2... | collective-permute-start | bytes 393224 | tf_op jit(solution)/shard_map/ppermute | solution.py:401
  7.5 5.5 %collective-permute-start.1 = (bf16[256,256]{1,0:T(8,128)(2,1)S(1)}, bf16[256,256]{1,0:T(8,128)(2,1)S(1)}, u32[]{:S(2)}, u32[]{:S(2)}) collective-permute-start(bf16[256,256]{1,0:T(8,128)(2,1)S(1)} %load.1.refs_0_), channel_id=1, source_target_pairs={{0,6},{10,14},{1,7},{11,15},{16,22},{26,30},{17,23},{27,31}} | collective-permute-start | bytes 393224 | tf_op jit(solution)/shard_map/ppermute | solution.py:401
  11.4 1.8 %collective-permute-start.3 = (bf16[256,256]{1,0:T(8,128)(2,1)S(1)}, bf16[256,256]{1,0:T(8,128)(2,1)S(1)}, u32[]{:S(2)}, u32[]{:S(2)}) collective-permute-start(bf16[256,256]{1,0:T(8,128)(2,1)S(1)} %pick.3.refs_0_), channel_id=1, source_target_pairs={{0,1},{1,0},{2,3},{3,2},{4,5},{5,4},{6,7},{7,6},{8,9},{9,8},{10,11... | collective-permute-start | bytes 393224 | tf_op jit(solution)/shard_map/ppermute | solution.py:393
  13.0 1.4 %collective-permute-start.2 = (bf16[256,256]{1,0:T(8,128)(2,1)S(1)}, bf16[256,256]{1,0:T(8,128)(2,1)S(1)}, u32[]{:S(2)}, u32[]{:S(2)}) collective-permute-start(bf16[256,256]{1,0:T(8,128)(2,1)S(1)} %pick.2.refs_2_), channel_id=1, source_target_pairs={{0,1},{1,0},{2,3},{3,2},{4,5},{5,4},{6,7},{7,6},{8,9},{9,8},{10,11... | collective-permute-start | bytes 393224 | tf_op jit(solution)/shard_map/ppermute | solution.py:393
  15.2 3.8 %collective-permute-start.4 = (f32[12,256]{1,0:T(8,128)S(1)}, f32[12,256]{1,0:T(8,128)S(1)}, u32[]{:S(2)}, u32[]{:S(2)}) collective-permute-start(f32[12,256]{1,0:T(8,128)S(1)} %get-tuple-element.40.refs_0_.refs_7_), channel_id=1, source_target_pairs={{0,8},{8,0},{16,24},{24,16},{1,9},{9,1},{17,25},{25,17},{2,10},{10... | collective-permute-start | bytes 36872 | tf_op jit(solution)/shard_map/ppermute | solution.py:390
  20.6 1.6 %collective-permute-start.6 = (bf16[512,256]{1,0:T(8,128)(2,1)S(1)}, bf16[512,256]{1,0:T(8,128)(2,1)S(1)}, u32[]{:S(2)}, u32[]{:S(2)}) collective-permute-start(bf16[512,256]{1,0:T(8,128)(2,1)S(1)} %get-tuple-element.49), channel_id=1, source_target_pairs={{0,1},{1,0},{2,3},{3,2},{4,5},{5,4},{6,7},{7,6},{8,9},{9,8},{10,11... | collective-permute-start | bytes 786440 | tf_op jit(solution)/shard_map/ppermute | solution.py:393
  20.7 5.9 %collective-permute-start.5 = (bf16[256,256]{1,0:T(8,128)(2,1)S(1)}, bf16[256,256]{1,0:T(8,128)(2,1)S(1)}, u32[]{:S(2)}, u32[]{:S(2)}) collective-permute-start(bf16[256,256]{1,0:T(8,128)(2,1)S(1)} %get-tuple-element.42), channel_id=1, source_target_pairs={{0,8},{8,0},{16,24},{24,16},{1,9},{9,1},{17,25},{25,17},{2,10},{10... | collective-permute-start | bytes 393224 | tf_op jit(solution)/shard_map/ppermute | solution.py:390
  22.2 5.6 %collective-permute-start.8 = (bf16[256,256]{1,0:T(8,128)(2,1)S(1)}, bf16[256,256]{1,0:T(8,128)(2,1)S(1)}, u32[]{:S(2)}, u32[]{:S(2)}) collective-permute-start(bf16[256,256]{1,0:T(8,128)(2,1)S(1)} %get-tuple-element.55), channel_id=1, source_target_pairs={{0,16},{8,24},{16,0},{24,8},{1,17},{9,25},{17,1},{25,9},{2,18},{10... | collective-permute-start | bytes 393224 | tf_op jit(solution)/shard_map/ppermute | solution.py:390
  24.3 11.3 %collective-permute-start.7 = (bf16[256,256]{1,0:T(8,128)(2,1)S(1)}, bf16[256,256]{1,0:T(8,128)(2,1)S(1)}, u32[]{:S(2)}, u32[]{:S(2)}) collective-permute-start(bf16[256,256]{1,0:T(8,128)(2,1)S(1)} %get-tuple-element.52), channel_id=1, source_target_pairs={{0,8},{8,0},{16,24},{24,16},{1,9},{9,1},{17,25},{25,17},{2,10},{10... | collective-permute-start | bytes 393224 | tf_op jit(solution)/shard_map/ppermute | solution.py:390
  27.9 8.6 %collective-permute-start.9 = (bf16[64,256]{1,0:T(8,128)(2,1)S(1)}, bf16[64,256]{1,0:T(8,128)(2,1)S(1)}, u32[]{:S(2)}, u32[]{:S(2)}) collective-permute-start(bf16[64,256]{1,0:T(8,128)(2,1)S(1)} %get-tuple-element.58), channel_id=1, source_target_pairs={{6,0},{7,1},{0,2},{1,3},{2,4},{3,5},{14,8},{15,9},{8,10},{9,11},{1... | collective-permute-start | bytes 98312 | tf_op jit(solution)/shard_map/ppermute | solution.py:405
  30.5 5.9 %collective-permute-start.10 = (bf16[64,256]{1,0:T(8,128)(2,1)S(1)}, bf16[64,256]{1,0:T(8,128)(2,1)S(1)}, u32[]{:S(2)}, u32[]{:S(2)}) collective-permute-start(bf16[64,256]{1,0:T(8,128)(2,1)S(1)} %get-tuple-element.59), channel_id=1, source_target_pairs={{4,0},{5,1},{6,2},{7,3},{0,4},{1,5},{2,6},{3,7},{12,8},{13,9},{14,... | collective-permute-start | bytes 98312 | tf_op jit(solution)/shard_map/ppermute | solution.py:405
  31.5 5.1 %collective-permute-start.11 = (bf16[64,256]{1,0:T(8,128)(2,1)S(1)}, bf16[64,256]{1,0:T(8,128)(2,1)S(1)}, u32[]{:S(2)}, u32[]{:S(2)}) collective-permute-start(bf16[64,256]{1,0:T(8,128)(2,1)S(1)} %get-tuple-element.60), channel_id=1, source_target_pairs={{2,0},{3,1},{4,2},{5,3},{6,4},{7,5},{0,6},{1,7},{10,8},{11,9},{12,... | collective-permute-start | bytes 98312 | tf_op jit(solution)/shard_map/ppermute | solution.py:405
  35.0 1.6 %collective-permute-start.12 = (bf16[64,256]{1,0:T(8,128)(2,1)S(1)}, bf16[64,256]{1,0:T(8,128)(2,1)S(1)}, u32[]{:S(2)}, u32[]{:S(2)}) collective-permute-start(bf16[64,256]{1,0:T(8,128)(2,1)S(1)} %get-tuple-element.61), channel_id=1, source_target_pairs={{4,6},{5,7},{12,14},{13,15},{20,22},{21,23},{28,30},{29,31}} | collective-permute-start | bytes 98312 | tf_op jit(solution)/shard_map/ppermute | solution.py:405
